TPU v7x, 256 devices: a whole 4x4x8 slice. The times are simulated.
256 devices in a mesh: prow: 8 (over y, x_lo), pcol: 32 (over z, x_hi, core).
Axes of the slice: x: 4 (x_hi: 2, x_lo: 2; x = x_hi * 2 + x_lo), y: 4, z: 8, core: 2. Of those that a mesh axis runs over, the one named last changes fastest.
Arguments:
- pair: bfloat16 [768, 768, 128], P('prow', 'pcol'), may hold values from -6 to 6
- pair_mask: int32 [768, 768], P('prow', 'pcol'), may hold values 0 or 1
- in_gain: float32 [128], replicated, may hold values from 0.1 to 1.9
- in_bias: float32 [128], replicated, may hold values from -3 to 3
- input_proj: bfloat16 [128, 512], replicated, may hold values from -0.5 to 0.5
- gate_weight: bfloat16 [128, 128], replicated, may hold values from -0.5 to 0.5
- out_gain: float32 [128], replicated, may hold values from 0.1 to 1.9
- out_bias: float32 [128], replicated, may hold values from -3 to 3
- out_weight: bfloat16 [128, 128], replicated, may hold values from -0.5 to 0.5
Outputs:
- update: bfloat16 [768, 768, 128], P('prow', 'pcol')
All inputs are finite; a program needn't handle non-finite values. No bound on the sum of `pair_mask` on one device may be relied on, other than what follows from the above.
Results may differ from a plain program's by a relative error of at most 0.0053.
Values may be sent and summed in bfloat16 or wider, within the bound.
No kernel may reach another device: no remote copies, remote signals or barrier semaphores. Data moves between devices by JAX's collectives and lax.ppermute only.
A program may use at most 128 MiB of HBM per device.

v0:
```python
import jax
import jax.numpy as jnp
from jax import lax
from jax.sharding import PartitionSpec as P


def layer_norm(values, gain, bias):
    mean = jnp.mean(values, axis=-1, keepdims=True)
    centred = values - mean
    var = jnp.mean(centred * centred, axis=-1, keepdims=True)
    return centred * lax.rsqrt(var + 1e-05) * gain + bias


def body(
    pair, pair_mask, in_gain, in_bias, input_proj, gate_weight, out_gain, out_bias, out_weight
):
    rows_here, cols_here, width = pair.shape
    normed_in = layer_norm(pair.astype(jnp.float32), in_gain, in_bias).astype(jnp.bfloat16)
    flat = normed_in.reshape(rows_here * cols_here, width)
    proj = jnp.dot(flat, input_proj, preferred_element_type=jnp.float32).reshape(
        rows_here, cols_here, 4 * width
    )
    live = pair_mask.astype(jnp.float32)[:, :, None]
    left = (live * jax.nn.sigmoid(proj[:, :, :width]) * proj[:, :, width : 2 * width]).astype(
        jnp.bfloat16
    )
    right = (
        live * jax.nn.sigmoid(proj[:, :, 2 * width : 3 * width]) * proj[:, :, 3 * width :]
    ).astype(jnp.bfloat16)
    right_all = lax.all_gather(right, "prow", axis=0, tiled=True)
    right_mine = lax.all_to_all(right_all, "pcol", split_axis=0, concat_axis=1, tiled=True)
    tri = jnp.einsum(
        "ikc,jkc->ijc",
        lax.all_gather(left, "pcol", axis=1, tiled=True),
        right_mine,
        preferred_element_type=jnp.float32,
    )
    normed_tri = layer_norm(tri, out_gain, out_bias).astype(jnp.bfloat16)
    gate = jax.nn.sigmoid(jnp.dot(flat, gate_weight, preferred_element_type=jnp.float32))
    mixed = jnp.dot(
        normed_tri.reshape(rows_here * cols_here, width),
        out_weight,
        preferred_element_type=jnp.float32,
    )
    return (gate * mixed).reshape(rows_here, cols_here, width).astype(jnp.bfloat16)


def solution(mesh):
    return jax.shard_map(
        body,
        mesh=mesh,
        in_specs=(P("prow", "pcol", None), P("prow", "pcol"), P(), P(), P(), P(), P(), P(), P()),
        out_specs=P("prow", "pcol", None),
        check_vma=False,
    )
```

profile of v0, /device:TPU:32, one launch (start us, length us, event | category | flops | bytes accessed | tf_op | source)
XLA Modules:
  0.0 414.6 jit_solution(10919002142035566365)
XLA Ops:
  6.5 0.0 all-gather.3.cloned.1.call-start
  6.6 1.5 convert_reduce_fusion
  8.1 0.1 copy.44
  8.2 0.1 copy.45
  8.3 0.7 fusion.6
  9.0 0.1 copy.46
  9.1 0.1 copy.47
  9.2 0.1 copy.48
  9.3 0.8 fusion.9
  10.1 0.8 fusion.20
  10.9 1.6 fusion.10
  12.4 0.0 all-gather.3.cloned.1.call-update
  12.5 0.0 all-gather.5.cloned.1.call-start
  12.5 0.7 all-gather.5.cloned.1.call-update
  13.2 105.0 %all-gather.3.cloned.1.call-done = bf16[768,24,128]{2,1,0:T(8,128)(2,1)} async-done(((bf16[96,24,128]{2,1,0:T(8,128)(2,1)}), bf16[768,24,128]{2,1,0:T(8,128)(2,1)}) %all-gather.3.cloned.1.call-update) | async-done | bytes 4718608 | tf_op jit(solution)/shard_map/all_gather | solution.py:30
  118.2 9.8 %all-to-all-start = ((bf16[768,24,128]{2,1,0:T(8,128)(2,1)}), bf16[768,24,128]{2,1,0:T(8,128)(2,1)}, u32[]{:S(2)}, u32[]{:S(2)}) async-start(bf16[768,24,128]{2,1,0:T(8,128)(2,1)} %all-gather.3.cloned.1.call-done), calls=%async_computation | async-start | bytes 9437184 | tf_op jit(solution)/shard_map/all_to_all | solution.py:31
  128.0 0.5 fusion.2
  128.5 128.4 %all-to-all-done = bf16[768,24,128]{2,1,0:T(8,128)(2,1)} async-done(((bf16[768,24,128]{2,1,0:T(8,128)(2,1)}), bf16[768,24,128]{2,1,0:T(8,128)(2,1)}, u32[]{:S(2)}, u32[]{:S(2)}) %all-to-all-start) | async-done | bytes 4718624 | tf_op jit(solution)/shard_map/all_to_all | solution.py:31
  256.9 5.9 %copy.49 = bf16[24,32,24,128]{3,2,1,0:T(8,128)(2,1)} copy(bf16[24,32,24,128]{3,2,0,1:T(8,128)(2,1)} %bitcast.3) | data formatting | bytes 9437184 | tf_op jit(solution)/shard_map/all_to_all | solution.py:31
  262.8 7.2 %copy.50 = bf16[24,768,128]{1,0,2:T(8,128)(2,1)} copy(bf16[24,768,128]{2,1,0:T(8,128)(2,1)} %bitcast.24) | data formatting | bytes 9437184 | tf_op jit(solution)/shard_map/all_to_all | solution.py:31
  270.0 90.4 %all-gather.5.cloned.1.call-done = bf16[96,768,128]{2,1,0:T(8,128)(2,1)} async-done(((bf16[96,24,128]{2,1,0:T(8,128)(2,1)}), bf16[96,768,128]{2,1,0:T(8,128)(2,1)}) %all-gather.5.cloned.1.call-update) | async-done | bytes 18874384 | tf_op jit(solution)/shard_map/all_gather | solution.py:34
  360.4 32.7 %copy.51 = bf16[96,768,128]{0,1,2:T(8,128)(2,1)} copy(bf16[96,768,128]{2,1,0:T(8,128)(2,1)} %all-gather.5.cloned.1.call-done) | data formatting | bytes 37748736 | tf_op jit(solution)/shard_map/all_gather | solution.py:34
  393.1 11.8 %bitcast_reduce_fusion = (f32[96,24]{0,1:T(8,128)S(1)}, f32[128,24,96]{2,1,0:T(8,128)S(1)}) fusion(bf16[24,768,128]{1,0,2:T(8,128)(2,1)} %copy.50, bf16[96,768,128]{0,1,2:T(8,128)(2,1)} %copy.51), kind=kOutput, calls=%fused_computation.7 | convolution fusion | flops 453277440 | bytes 24781824 | tf_op jit(solution)/shard_map/ikc,jkc->ijc/dot_general | solution.py:32
  404.9 0.0 copy-start.7
  404.9 0.3 multiply_reduce_fusion
  405.2 0.3 copy-done.7
  405.5 0.0 copy-done.8
  405.6 0.3 add_convert_fusion
  405.9 0.0 copy-start.3
  405.9 0.6 copy.52
  406.6 0.1 copy-done.3
  406.7 1.1 fusion.3
  (20 shorter events, 0.1 us)
Async XLA Ops:
  6.5 3.6 copy-start
  6.5 1.7 copy-start.2
  6.5 2.6 copy-start.4
  6.5 2.7 copy-start.6
  6.5 2.7 copy-start.5
  6.5 111.6 %all-gather.3.cloned.1.call-start = ((), (), s32[]{:S(2)}) async-start(), calls=%async_computation.1 | async-start | bytes 5308416 | tf_op jit(solution)/shard_map/all_gather | solution.py:30
  12.5 348.0 %all-gather.5.cloned.1.call-start = ((), (), s32[]{:S(2)}) async-start(), calls=%async_computation.2 | async-start | bytes 19464192 | tf_op jit(solution)/shard_map/all_gather | solution.py:34
  13.2 114.8 %copy-start.9 = (bf16[128,128]{1,0:T(8,128)(2,1)S(1)}, bf16[128,128]{1,0:T(8,128)(2,1)}, u32[]{:S(2)}) copy-start(bf16[128,128]{1,0:T(8,128)(2,1)} %param.14) | copy-start | bytes 98308
  118.2 138.7 %all-to-all-start = ((bf16[768,24,128]{2,1,0:T(8,128)(2,1)}), bf16[768,24,128]{2,1,0:T(8,128)(2,1)}, u32[]{:S(2)}, u32[]{:S(2)}) async-start(bf16[768,24,128]{2,1,0:T(8,128)(2,1)} %all-gather.3.cloned.1.call-done), calls=%async_computation | async-start | bytes 9437184 | tf_op jit(solution)/shard_map/all_to_all | solution.py:31
  404.9 0.7 copy-start.7
  404.9 0.7 copy-start.8
  405.9 0.8 copy-start.3
  406.6 1.2 copy-start.1
Sparse Core Ops, SparseCore 0:
  12.6 105.5 all-gather.2
  120.8 239.6 all-gather.4
where the time goes:
time: 418 us; the launch traced here: 415 us
  waiting for transfers between devices  325 us (78%)
  local copies, waits for them, and re-layouts  47.3 us (11%)
  matrix products  14.1 us (3%)
  between operations  13.6 us (3%)
  starting transfers between devices  9.89 us (2%)
  other arithmetic  5.21 us (1%)
    all_to_all x1, waiting for transfers between devices, body(): lax.all_to_all(right_all, 'pcol', split_axis=0, concat_axis=1, tiled=True)  128 us
    all_gather x1, waiting for transfers between devices, body(): right_all = lax.all_gather(right, 'prow', axis=0, tiled=True)  105 us
    all_gather x1, waiting for transfers between devices, body(): lax.all_gather(left, 'pcol', axis=1, tiled=True)  90.4 us
    all_gather x1, local copies, waits for them, and re-layouts, body(): lax.all_gather(left, 'pcol', axis=1, tiled=True)  32.7 us
    all_to_all x2, local copies, waits for them, and re-layouts, body(): lax.all_to_all(right_all, 'pcol', split_axis=0, concat_axis=1, tiled=True)  13.1 us
    dot_general x1, matrix products, body(): jnp.einsum('ikc,jkc->ijc', lax.all_gather(left, 'pcol', axis=1, tiled=Tru...  11.8 us
    all_to_all x1, starting transfers between devices, body(): lax.all_to_all(right_all, 'pcol', split_axis=0, concat_axis=1, tiled=True)  9.81 us
  transfers between devices with their start and end apart: 3, of which 3 were waited for; matrix products, arithmetic and copies ran while one was open for 3% of the time, Pallas kernels for 0%

commit v1 on v0

v1 whole, which is shorter than its diff:
```python
import jax
import jax.numpy as jnp
from jax import lax
from jax.sharding import Mesh
from jax.sharding import PartitionSpec as P

CHIPS = ("y", "xl", "z", "xh")


def layer_norm(values, gain, bias):
    mean = jnp.mean(values, axis=-1, keepdims=True)
    centred = values - mean
    var = jnp.mean(centred * centred, axis=-1, keepdims=True)
    return centred * lax.rsqrt(var + 1e-05) * gain + bias


def body(
    pair, pair_mask, in_gain, in_bias, input_proj, gate_weight, out_gain, out_bias, out_weight
):
    rows, cols, width = pair.shape
    normed_in = layer_norm(pair.astype(jnp.float32), in_gain, in_bias).astype(jnp.bfloat16)
    flat = normed_in.reshape(rows * cols, width)
    proj = jnp.dot(flat, input_proj, preferred_element_type=jnp.float32).reshape(
        rows, cols, 4 * width
    )
    live = pair_mask.astype(jnp.float32)[:, :, None]
    left = (live * jax.nn.sigmoid(proj[:, :, :width]) * proj[:, :, width : 2 * width]).astype(
        jnp.bfloat16
    )
    right = (
        live * jax.nn.sigmoid(proj[:, :, 2 * width : 3 * width]) * proj[:, :, 3 * width :]
    ).astype(jnp.bfloat16)
    both = jnp.stack([left, right]).transpose(3, 0, 2, 1)
    both = both.reshape(width, 2 * rows * cols // 128, 128)
    both = lax.all_to_all(both, CHIPS, 0, 0, tiled=True)
    both = both.reshape(8, 16, 2, cols, rows)
    left, right = both[:, :, 0], both[:, :, 1]
    part = jnp.einsum("pqki,rqkj->pirj", left, right, preferred_element_type=jnp.float32)
    part = part.reshape(8, rows, 16, 2, cols)
    core = lax.axis_index("core")
    mine = lax.dynamic_index_in_dim(part, core, 3, keepdims=False)
    other = lax.dynamic_index_in_dim(part, 1 - core, 3, keepdims=False)
    got = lax.ppermute(other, "core", [(0, 1), (1, 0)])
    tri = (mine + got).astype(jnp.bfloat16)
    tri = tri.transpose(0, 2, 1, 3).reshape(width, rows * cols // 128, 128)
    tri = lax.all_to_all(tri, CHIPS, 0, 0, tiled=True)
    tri = tri.reshape(width, rows * cols).T.astype(jnp.float32)
    normed_tri = layer_norm(tri, out_gain, out_bias).astype(jnp.bfloat16)
    gate = jax.nn.sigmoid(jnp.dot(flat, gate_weight, preferred_element_type=jnp.float32))
    mixed = jnp.dot(normed_tri, out_weight, preferred_element_type=jnp.float32)
    return (gate * mixed).reshape(rows, cols, width).astype(jnp.bfloat16)


def solution(mesh):
    fine = Mesh(mesh.devices.reshape(4, 2, 8, 2, 2), ("y", "xl", "z", "xh", "core"))
    split = P(("y", "xl"), ("z", "xh", "core"))
    return jax.shard_map(
        body,
        mesh=fine,
        in_specs=(split, split, P(), P(), P(), P(), P(), P(), P()),
        out_specs=split,
        check_vma=False,
    )
```

time: 418 us -> 134 us (0.32)
  waiting for transfers between devices: 325 us -> 65 us
  local copies, waits for them, and re-layouts: 47.3 us -> 30.9 us
  between operations: 13.6 us -> 0.3 us
  starting transfers between devices: 9.89 us -> 21.9 us
  matrix products: 14.1 us -> 5.9 us
  other arithmetic: 5.21 us -> 9.65 us
    all_gather x2 -> x0, waiting for transfers between devices: 195 us -> none  [the longest x1 105 us: body(): right_all = lax.all_gather(right, 'prow', axis=0, tiled=True)]
    all_to_all x1 -> x2, waiting for transfers between devices: 128 us -> 61.3 us  [the longest x1 36.2 us: body(): both = lax.all_to_all(both, CHIPS, 0, 0, tiled=True)]
    all_gather x1 -> x0, local copies, waits for them, and re-layouts: 32.7 us -> none  [body(): lax.all_gather(left, 'pcol', axis=1, tiled=True)]
    dot_general x0 -> x4, local copies, waits for them, and re-layouts: none -> 15.3 us  [body(): jnp.einsum('pqki,rqkj->pirj', left, right, preferred_element_type=jnp.flo...]
    all_to_all x2 -> x0, local copies, waits for them, and re-layouts: 13.1 us -> none  [body(): lax.all_to_all(right_all, 'pcol', split_axis=0, concat_axis=1, tiled=True)]
    all_to_all x1 -> x2, starting transfers between devices: 9.81 us -> 21.9 us  [the longest x1 15 us: body(): both = lax.all_to_all(both, CHIPS, 0, 0, tiled=True)]
    reshape x0 -> x3, local copies, waits for them, and re-layouts: none -> 8.55 us  [the longest x1 5.57 us: body(): tri = tri.transpose(0, 2, 1, 3).reshape(width, rows * cols // 128, 128)]
    dot_general x2, matrix products: 12.9 us -> 4.7 us  [the longest x1 3.58 us: body(): jnp.einsum('pqki,rqkj->pirj', left, right, preferred_element_type=jnp.flo...]
  transfers between devices with their start and end apart: 3 -> 3, of which waited for: 3 -> 3; matrix products, arithmetic and copies ran while one was open for 3% -> 0% of each run, Pallas kernels for 0% -> 0%
where the time goes in v1:
time: 134 us
  waiting for transfers between devices  65 us (49%)
  local copies, waits for them, and re-layouts  30.9 us (23%)
  starting transfers between devices  21.9 us (16%)
  other arithmetic  9.65 us (7%)
  matrix products  5.9 us (4%)
    all_to_all x1, waiting for transfers between devices, body(): both = lax.all_to_all(both, CHIPS, 0, 0, tiled=True)  36.2 us
    all_to_all x1, waiting for transfers between devices, body(): tri = lax.all_to_all(tri, CHIPS, 0, 0, tiled=True)  25 us
    dot_general x4, local copies, waits for them, and re-layouts, body(): jnp.einsum('pqki,rqkj->pirj', left, right, preferred_element_type=jnp.flo...  15.3 us
    all_to_all x1, starting transfers between devices, body(): both = lax.all_to_all(both, CHIPS, 0, 0, tiled=True)  15 us
    all_to_all x1, starting transfers between devices, body(): tri = lax.all_to_all(tri, CHIPS, 0, 0, tiled=True)  6.87 us
    reshape x1, local copies, waits for them, and re-layouts, body(): tri = tri.transpose(0, 2, 1, 3).reshape(width, rows * cols // 128, 128)  5.57 us
    ppermute x1, waiting for transfers between devices, body(): got = lax.ppermute(other, 'core', [(0, 1), (1, 0)])  3.75 us
    dot_general x1, matrix products, body(): jnp.einsum('pqki,rqkj->pirj', left, right, preferred_element_type=jnp.flo...  3.58 us
  transfers between devices with their start and end apart: 3, of which 3 were waited for; matrix products, arithmetic and copies ran while one was open for 0% of the time, Pallas kernels for 0%

profile of v1, /device:TPU:32, one launch (start us, length us, event | category | flops | bytes accessed | tf_op | source)
XLA Modules:
  0.0 133.6 jit_solution(8335113801651726165)
XLA Ops:
  0.0 1.5 %convert_reduce_fusion = f32[96,24]{1,0:T(8,128)S(1)} fusion(bf16[96,24,128]{2,1,0:T(8,128)(2,1)} %param.9), kind=kLoop, calls=%fused_computation.13 | loop fusion | flops 587520 | bytes 599040 | tf_op jit(solution)/shard_map/reduce_sum | solution.py:11
  1.6 1.8 %fusion.12 = f32[96,24]{1,0:T(8,128)S(1)} fusion(bf16[96,24,128]{2,1,0:T(8,128)(2,1)} %param.9, f32[96,24]{1,0:T(8,128)S(1)} %broadcast_multiply_fusion), kind=kLoop, calls=%fused_computation.16 | loop fusion | flops 1177344 | bytes 608256 | tf_op jit(solution)/shard_map/reduce_sum | solution.py:13
  3.4 0.1 copy.26
  3.5 0.8 fusion.15
  4.3 0.8 copy-done.3
  5.1 0.8 fusion.29
  5.9 0.8 fusion.27
  6.7 0.1 maximum_bitcast_fusion
  6.8 0.2 copy.27
  6.9 1.9 %copy.28 = bf16[128,36,128]{2,1,0:T(8,128)(2,1)} copy(bf16[128,36,128]{0,2,1:T(8,128)(2,1)S(1)} %bitcast.62) | data formatting | bytes 2359296 | tf_op jit(solution)/shard_map/reshape | solution.py:34
  8.8 15.0 %all-to-all-start = ((bf16[128,36,128]{2,1,0:T(8,128)(2,1)}), bf16[128,36,128]{2,1,0:T(8,128)(2,1)S(1)}, u32[]{:S(2)}, u32[]{:S(2)}) async-start(bf16[128,36,128]{2,1,0:T(8,128)(2,1)} %copy.28), calls=%async_computation | async-start | bytes 2621440 | tf_op jit(solution)/shard_map/all_to_all | solution.py:35
  23.8 36.2 %all-to-all-done = bf16[128,36,128]{2,1,0:T(8,128)(2,1)S(1)} async-done(((bf16[128,36,128]{2,1,0:T(8,128)(2,1)}), bf16[128,36,128]{2,1,0:T(8,128)(2,1)S(1)}, u32[]{:S(2)}, u32[]{:S(2)}) %all-to-all-start) | async-done | bytes 1179680 | tf_op jit(solution)/shard_map/all_to_all | solution.py:35
  60.1 1.1 reshape.55
  61.2 0.1 slice_bitcast_fusion
  61.3 1.1 copy-done.2
  62.3 1.4 %copy.30 = bf16[8,96,24,16]{1,0,3,2:T(8,128)(2,1)} copy(bf16[8,96,24,16]{1,2,3,0:T(8,128)(2,1)S(1)} %slice_bitcast_fusion) | data formatting | bytes 1179648 | tf_op jit(solution)/shard_map/pqki,rqkj->pirj/dot_general | solution.py:38
  63.8 6.8 %dot_general.19 = bf16[16,2,24,24,16]{2,1,0,4,3:T(2,128)(2,1)S(1)} reshape(bf16[8,96,24,16]{1,0,3,2:T(8,128)(2,1)} %copy.30) | data formatting | bytes 1179648 | tf_op jit(solution)/shard_map/pqki,rqkj->pirj/dot_general | solution.py:38
  70.6 7.0 %copy.31 = bf16[16,2,24,24,16]{3,2,4,1,0:T(8,128)(2,1)} copy(bf16[16,2,24,24,16]{2,1,0,4,3:T(2,128)(2,1)S(1)} %dot_general.19) | data formatting | bytes 1179648 | tf_op jit(solution)/shard_map/pqki,rqkj->pirj/dot_general | solution.py:38
  77.6 3.6 %fusion.6 = f32[8,96,16,2,24]{1,4,3,2,0:T(8,128)S(1)} fusion(bf16[16,2,24,24,16]{3,2,4,1,0:T(8,128)(2,1)} %copy.31, bf16[8,16,2,24,96]{4,3,2,1,0:T(8,128)(2,1)} %copy-done.2), kind=kOutput, calls=%fused_computation.8 | convolution fusion | flops 452984832 | bytes 6291456 | tf_op jit(solution)/shard_map/pqki,rqkj->pirj/dot_general | solution.py:38
  81.2 1.3 dynamic-slice_bitcast_fusion
  82.5 3.7 %collective-permute-done = f32[8,96,16,24]{1,3,2,0:T(8,128)} collective-permute-done((f32[8,96,16,24]{1,3,2,0:T(8,128)}, f32[8,96,16,24]{1,3,2,0:T(8,128)}, u32[]{:S(2)}, u32[]{:S(2)}) %collective-permute-start) | collective-permute-done | bytes 1179680 | tf_op jit(solution)/shard_map/ppermute | solution.py:43
  86.2 2.5 %fusion.26 = bf16[8,16,96,24]{2,3,1,0:T(8,128)(2,1)} fusion(f32[8,96,16,24]{1,3,2,0:T(8,128)} %collective-permute-done, f32[8,96,16,2,24]{1,4,3,2,0:T(8,128)S(1)} %fusion.6, s32[]{:T(128)S(6)} %select_n.7), kind=kLoop, calls=%fused_computation.38 | loop fusion | flops 589824 | bytes 2949124 | tf_op jit(solution)/shard_map/transpose | solution.py:45
  88.7 3.1 %copy.32 = bf16[8,16,96,24]{3,2,1,0:T(8,128)(2,1)S(1)} copy(bf16[8,16,96,24]{2,3,1,0:T(8,128)(2,1)} %fusion.26) | data formatting | bytes 1179648 | tf_op jit(solution)/shard_map/transpose | solution.py:45
  91.8 5.6 %reshape.56 = bf16[128,18,128]{2,1,0:T(8,128)(2,1)} reshape(bf16[8,16,96,24]{3,2,1,0:T(8,128)(2,1)S(1)} %copy.32) | data formatting | bytes 1179648 | tf_op jit(solution)/shard_map/reshape | solution.py:45
  97.4 6.9 %all-to-all-start.1 = ((bf16[128,18,128]{2,1,0:T(8,128)(2,1)}), bf16[128,18,128]{2,1,0:T(8,128)(2,1)S(1)}, u32[]{:S(2)}, u32[]{:S(2)}) async-start(bf16[128,18,128]{2,1,0:T(8,128)(2,1)} %reshape.56), calls=%async_computation.1 | async-start | bytes 1572864 | tf_op jit(solution)/shard_map/all_to_all | solution.py:46
  104.3 0.5 fusion.2
  104.7 25.0 %all-to-all-done.1 = bf16[128,18,128]{2,1,0:T(8,128)(2,1)S(1)} async-done(((bf16[128,18,128]{2,1,0:T(8,128)(2,1)}), bf16[128,18,128]{2,1,0:T(8,128)(2,1)S(1)}, u32[]{:S(2)}, u32[]{:S(2)}) %all-to-all-start.1) | async-done | bytes 589856 | tf_op jit(solution)/shard_map/all_to_all | solution.py:46
  129.8 0.2 convert_reduce_fusion.1
  130.0 0.4 copy.33
  130.4 0.7 multiply_reduce_fusion
  131.1 1.3 %add_convert_fusion = bf16[128,2304]{0,1:T(8,128)(2,1)S(1)} fusion(f32[128,18,128]{0,2,1:T(8,128)S(1)} %copy.33, f32[128]{0:T(128)S(1)} %copy-done.9, f32[128]{0:T(128)S(1)} %copy-done.10, f32[2304]{0:T(1024)S(1)} %add_rsqrt_fusion.1, f32[2304]{0:T(1024)S(1)} %multiply_bitcast_fusion), kind=kLoop, calls=%fused_computation.36 | loop fusion | flops 1474560 | bytes 1788928 | tf_op jit(solution)/shard_map/convert_element_type | solution.py:48
  132.5 1.1 fusion.3
  (28 shorter events, 0.1 us)
Async XLA Ops:
  0.0 5.1 %copy-start = (bf16[128,512]{1,0:T(8,128)(2,1)S(1)}, bf16[128,512]{1,0:T(8,128)(2,1)}, u32[]{:S(2)}) copy-start(bf16[128,512]{1,0:T(8,128)(2,1)} %param.13) | copy-start | bytes 393220
  0.0 3.5 %copy-start.1 = (bf16[96,24,128]{2,1,0:T(8,128)(2,1)S(1)}, bf16[96,24,128]{2,1,0:T(8,128)(2,1)}, u32[]{:S(2)}) copy-start(bf16[96,24,128]{2,1,0:T(8,128)(2,1)} %param.9) | copy-start | bytes 1769476
  0.0 3.4 %copy-start.6 = (s32[96,24]{0,1:T(8,128)S(1)}, s32[96,24]{0,1:T(8,128)}, u32[]{:S(2)}) copy-start(s32[96,24]{0,1:T(8,128)} %param.10) | copy-start | bytes 27652
  0.0 3.5 %copy-start.8 = (f32[128]{0:T(128)S(1)}, f32[128]{0:T(128)}, u32[]{:S(2)}) copy-start(f32[128]{0:T(128)} %param.11) | copy-start | bytes 1540
  0.0 3.5 %copy-start.7 = (f32[128]{0:T(128)S(1)}, f32[128]{0:T(128)}, u32[]{:S(2)}) copy-start(f32[128]{0:T(128)} %param.12) | copy-start | bytes 1540
  4.3 0.8 copy-start.3
  8.8 51.3 %all-to-all-start = ((bf16[128,36,128]{2,1,0:T(8,128)(2,1)}), bf16[128,36,128]{2,1,0:T(8,128)(2,1)S(1)}, u32[]{:S(2)}, u32[]{:S(2)}) async-start(bf16[128,36,128]{2,1,0:T(8,128)(2,1)} %copy.28), calls=%async_computation | async-start | bytes 2621440 | tf_op jit(solution)/shard_map/all_to_all | solution.py:35
  61.2 1.2 copy-start.2
  82.5 3.8 %collective-permute-start = (f32[8,96,16,24]{1,3,2,0:T(8,128)}, f32[8,96,16,24]{1,3,2,0:T(8,128)}, u32[]{:S(2)}, u32[]{:S(2)}) collective-permute-start(f32[8,96,16,24]{1,3,2,0:T(8,128)} %dynamic-slice_bitcast_fusion), channel_id=1, source_target_pairs={{0,1},{1,0},{2,3},{3,2},{4,5},{5,4},{6,7},{7,6},{8,9},{9,8},{10,11... | collective-permute-start | bytes 3538952 | tf_op jit(solution)/shard_map/ppermute | solution.py:43
  97.4 6.9 %copy-start.4 = (bf16[96,24,128]{2,1,0:T(8,128)(2,1)S(1)}, bf16[96,24,128]{2,1,0:T(8,128)(2,1)}, u32[]{:S(2)}) copy-start(bf16[96,24,128]{2,1,0:T(8,128)(2,1)} %copy-done.3) | copy-start | bytes 1769476
  97.4 6.9 %copy-start.11 = (bf16[128,128]{1,0:T(8,128)(2,1)S(1)}, bf16[128,128]{1,0:T(8,128)(2,1)}, u32[]{:S(2)}) copy-start(bf16[128,128]{1,0:T(8,128)(2,1)} %param.14) | copy-start | bytes 98308
  97.4 32.4 %all-to-all-start.1 = ((bf16[128,18,128]{2,1,0:T(8,128)(2,1)}), bf16[128,18,128]{2,1,0:T(8,128)(2,1)S(1)}, u32[]{:S(2)}, u32[]{:S(2)}) async-start(bf16[128,18,128]{2,1,0:T(8,128)(2,1)} %reshape.56), calls=%async_computation.1 | async-start | bytes 1572864 | tf_op jit(solution)/shard_map/all_to_all | solution.py:46
  129.9 1.2 copy-start.9
  130.0 1.2 copy-start.10
  131.1 1.4 %copy-start.5 = (bf16[128,128]{1,0:T(8,128)(2,1)S(1)}, bf16[128,128]{1,0:T(8,128)(2,1)}, u32[]{:S(2)}) copy-start(bf16[128,128]{1,0:T(8,128)(2,1)} %param.17) | copy-start | bytes 98308

commit v2 on v1

v2 whole, which is shorter than its diff:
```python
import jax
import jax.numpy as jnp
from jax import lax
from jax.experimental import pallas as pl
from jax.experimental.pallas import tpu as pltpu
from jax.sharding import Mesh
from jax.sharding import PartitionSpec as P

CHIPS = ("y", "xl", "z", "xh")
LIMIT = 48 * 1024 * 1024
ROWS = 96
COLS = 24
CH = 128
SENT = 40
ORDER = ((0, 56, 16), (16, 24, 24), (40, 72, 24), (64, 0, 24), (88, 48, 8), (96, 0, 24), (120, 48, 8))
BF = jnp.bfloat16
F32 = jnp.float32


def dot(a, b, ca, cb):
    return lax.dot_general(a, b, (((ca,), (cb,)), ((), ())), preferred_element_type=F32)


def project_kernel(pair, mask, gain, bias, weight, sent, normed, rows, out):
    for at in range(0, ROWS * COLS, 256):
        x = pair[pl.ds(at, 256), :].astype(F32)
        mean = jnp.mean(x, axis=-1, keepdims=True)
        centred = x - mean
        var = jnp.mean(centred * centred, axis=-1, keepdims=True)
        x = (centred * lax.rsqrt(var + 1e-05) * gain[...] + bias[...]).astype(BF)
        normed[pl.ds(at, 256), :] = x
        rows[pl.ds(at, 256), :] = x.astype(F32)

    lane = lax.broadcasted_iota(jnp.int32, (ROWS, CH), 1)
    token = lax.broadcasted_iota(jnp.int32, (ROWS, CH), 0)
    source = lane
    for start, first, count in ORDER:
        source = jnp.where((lane >= start) & (lane < start + count), lane - start + first, source)
    spread = (source == token).astype(F32).astype(BF)
    live = dot(mask[...].astype(F32).astype(BF), spread, 1, 0)

    turned = weight[...].astype(F32).T.astype(BF)
    at_lane = lax.broadcasted_iota(jnp.int32, (CH, CH), 1)

    def column(k):
        x = rows[pl.ds(k, ROWS, stride=COLS), :]
        x = jnp.concatenate([x[first : first + count] for _, first, count in ORDER], axis=0)
        x = x.astype(BF)
        proj = dot(turned, x, 1, 1)
        m = live[k : k + 1, :]
        left = m * jax.nn.sigmoid(proj[:CH]) * proj[CH : 2 * CH]
        right = m * jax.nn.sigmoid(proj[2 * CH : 3 * CH]) * proj[3 * CH :]
        out[pl.ds(k, CH, stride=SENT), :] = jnp.where(at_lane < ROWS, left, right)
        return right

    for k in range(8):
        low = column(k)
        high = column(k + 8)
        out[pl.ds(24 + k, CH, stride=SENT), :] = jnp.where(
            at_lane < 64, low, pltpu.roll(high, 64, 1)
        )
        out[pl.ds(32 + k, CH, stride=SENT), :] = column(k + 16)
    sent[...] = out[...].reshape(CH, SENT, CH).astype(BF)


def product_kernel(core, own, other, sent):
    shift = jnp.where(core[0] == 0, 32, 112)
    lane = lax.broadcasted_iota(jnp.int32, (384, CH), 1)
    lefts, rights = [], []
    for block in range(8):
        ls, rs = [], []
        for ref in (own, other):
            v = ref[pl.ds(block * 16, 16)].astype(F32)
            left = v[:, :24].reshape(384, CH)
            mid = v[:, 24:32]
            right = jnp.concatenate(
                [mid, pltpu.roll(mid, 64, 2), v[:, 32:40]], axis=1
            ).reshape(384, CH)
            right = jnp.where(lane < 64, right, left)
            rs.append(pltpu.roll(right, shift, 1))
            ls.append(left.astype(BF))
        lefts.append(jnp.concatenate(ls, axis=0))
        rights.append(jnp.concatenate(rs, axis=0))
    lane = lax.broadcasted_iota(jnp.int32, (768, CH), 1)
    left = jnp.concatenate(lefts, axis=1)
    for pair in range(4):
        right = jnp.where(lane < 64, rights[2 * pair], pltpu.roll(rights[2 * pair + 1], 64, 1))
        tri = dot(right.astype(BF).T, left, 1, 0).astype(BF)
        for part, at in enumerate((0, 24, 64, 88)):
            for block in range(8):
                sent[block * 16 + pair * 4 + part] = tri[
                    at : at + 24, block * CH : (block + 1) * CH
                ]


def finish_kernel(tri, gate, gain, bias, weight, update, cols, out):
    cols[...] = tri[...].astype(F32).reshape(CH * COLS, CH)
    for j in range(COLS):
        v = cols[pl.ds(j, CH, stride=COLS), :]
        mean = jnp.mean(v, axis=0, keepdims=True)
        centred = v - mean
        var = jnp.mean(centred * centred, axis=0, keepdims=True)
        v = (centred * lax.rsqrt(var + 1e-05) * gain[...] + bias[...]).astype(BF)
        mixed = dot(v, weight[...], 0, 0)
        place = {first: mixed[start : start + count] for start, first, count in ORDER[:5]}
        out[pl.ds(j, ROWS, stride=COLS), :] = jnp.concatenate(
            [place[first] for first in sorted(place)], axis=0
        )
    for at in range(0, ROWS * COLS, 256):
        here = pl.ds(at, 256)
        update[here, :] = (gate[here, :] * out[here, :]).astype(BF)


VMEM = pl.BlockSpec(memory_space=pltpu.VMEM)
SMEM = pl.BlockSpec(memory_space=pltpu.SMEM)
PARAMS = pltpu.CompilerParams(vmem_limit_bytes=LIMIT)


def body(
    pair, pair_mask, in_gain, in_bias, input_proj, gate_weight, out_gain, out_bias, out_weight
):
    tokens = ROWS * COLS
    sent, normed = pl.pallas_call(
        project_kernel,
        out_shape=(
            jax.ShapeDtypeStruct((CH, SENT, CH), BF),
            jax.ShapeDtypeStruct((tokens, CH), BF),
        ),
        in_specs=[VMEM] * 5,
        out_specs=(VMEM, VMEM),
        scratch_shapes=[pltpu.VMEM((tokens, CH), F32), pltpu.VMEM((CH * SENT, CH), F32)],
        compiler_params=PARAMS,
        name="project",
    )(
        pair.reshape(tokens, CH),
        pair_mask.T,
        in_gain.reshape(1, CH),
        in_bias.reshape(1, CH),
        input_proj,
    )
    own = lax.all_to_all(sent, CHIPS, 0, 0, tiled=True)
    other = lax.ppermute(own, "core", [(0, 1), (1, 0)])
    gate = jax.nn.sigmoid(jnp.dot(normed, gate_weight, preferred_element_type=F32))
    core = lax.axis_index("core").astype(jnp.int32).reshape(1)
    tri = pl.pallas_call(
        product_kernel,
        out_shape=jax.ShapeDtypeStruct((CH, COLS, CH), BF),
        in_specs=[SMEM, VMEM, VMEM],
        out_specs=VMEM,
        compiler_params=PARAMS,
        name="product",
    )(core, own, other)
    tri = lax.all_to_all(tri, CHIPS, 0, 0, tiled=True)
    update = pl.pallas_call(
        finish_kernel,
        out_shape=jax.ShapeDtypeStruct((tokens, CH), BF),
        in_specs=[VMEM] * 5,
        out_specs=VMEM,
        scratch_shapes=[pltpu.VMEM((CH * COLS, CH), F32), pltpu.VMEM((tokens, CH), F32)],
        compiler_params=PARAMS,
        name="finish",
    )(tri, gate, out_gain.reshape(CH, 1), out_bias.reshape(CH, 1), out_weight)
    return update.reshape(ROWS, COLS, CH)


def solution(mesh):
    fine = Mesh(mesh.devices.reshape(4, 2, 8, 2, 2), ("y", "xl", "z", "xh", "core"))
    split = P(("y", "xl"), ("z", "xh", "core"))
    return jax.shard_map(
        body,
        mesh=fine,
        in_specs=(split, split, P(), P(), P(), P(), P(), P(), P()),
        out_specs=split,
        check_vma=False,
    )
```

time: 134 us -> 99.5 us (0.74)
  blocking collectives: 0 us -> 51.1 us
  waiting for transfers between devices: 65 us -> 27.8 us
  local copies, waits for them, and re-layouts: 30.9 us -> 4.23 us
  starting transfers between devices: 21.9 us -> 6.87 us
  other arithmetic: 9.65 us -> 0 us
  Pallas kernels: 0 us -> 8.69 us
  matrix products: 5.9 us -> 0.46 us
    all_to_all x0 -> x1, blocking collectives: none -> 51.1 us  [body(): own = lax.all_to_all(sent, CHIPS, 0, 0, tiled=True)]
    all_to_all x1 -> x0, waiting for transfers between devices: 36.2 us -> none  [body(): both = lax.all_to_all(both, CHIPS, 0, 0, tiled=True)]
    dot_general x4 -> x0, local copies, waits for them, and re-layouts: 15.3 us -> none  [body(): jnp.einsum('pqki,rqkj->pirj', left, right, preferred_element_type=jnp.flo...]
    all_to_all x1 -> x0, starting transfers between devices: 15 us -> none  [body(): both = lax.all_to_all(both, CHIPS, 0, 0, tiled=True)]
    pallas_call x0 -> x3, Pallas kernels: none -> 8.69 us  [the longest x1 3.54 us: body(): pl.pallas_call(product_kernel, out_shape=jax.ShapeDtypeStruct((CH, COLS,...]
    reshape x3 -> x2, local copies, waits for them, and re-layouts: 8.55 us -> 0.23 us  [the longest x1 0.11 us: body(): out_gain.reshape(CH, 1)]
    dot_general x4 -> x1, matrix products: 5.9 us -> 0.46 us  [body(): jnp.dot(normed, gate_weight, preferred_element_type=F32)]
    reduce_sum x4 -> x0, other arithmetic: 4.13 us -> none  [the longest x2 2.46 us: layer_norm(): var = jnp.mean(centred * centred, axis=-1, keepdims=True)]
  transfers between devices with their start and end apart: 3 -> 2, of which waited for: 3 -> 2; matrix products, arithmetic and copies ran while one was open for 0% -> 1% of each run, Pallas kernels for 0% -> 0%
where the time goes in v2:
time: 99.5 us; the launch traced here: 99.2 us
  blocking collectives  51.1 us (51%)
  waiting for transfers between devices  27.8 us (28%)
  Pallas kernels  8.69 us (9%)
  starting transfers between devices  6.87 us (7%)
  local copies, waits for them, and re-layouts  4.23 us (4%)
    all_to_all x1, blocking collectives, body(): own = lax.all_to_all(sent, CHIPS, 0, 0, tiled=True)  51.1 us
    all_to_all x1, waiting for transfers between devices, body(): tri = lax.all_to_all(tri, CHIPS, 0, 0, tiled=True)  24.8 us
    all_to_all x1, starting transfers between devices, body(): tri = lax.all_to_all(tri, CHIPS, 0, 0, tiled=True)  6.87 us
    unnamed x18, local copies, waits for them, and re-layouts  4.01 us
    pallas_call x1, Pallas kernels, body(): pl.pallas_call(product_kernel, out_shape=jax.ShapeDtypeStruct((CH, COLS,...  3.54 us
    ppermute x1, waiting for transfers between devices, body(): other = lax.ppermute(own, 'core', [(0, 1), (1, 0)])  3.03 us
    pallas_call x1, Pallas kernels, body(): pl.pallas_call(finish_kernel, out_shape=jax.ShapeDtypeStruct((tokens, CH)...  2.71 us
    pallas_call x1, Pallas kernels, body(): pl.pallas_call(project_kernel, out_shape=(jax.ShapeDtypeStruct((CH, SENT,...  2.44 us
  transfers between devices with their start and end apart: 2, of which 2 were waited for; matrix products, arithmetic and copies ran while one was open for 1% of the time, Pallas kernels for 0%

profile of v2, /device:TPU:32, one launch (start us, length us, event | category | flops | bytes accessed | tf_op | source)
XLA Modules:
  0.0 99.2 jit_solution(12141090438358511458)
XLA Ops:
  0.0 0.0 copy-start
  0.0 0.0 copy-start.1
  0.0 1.1 %copy-done.1 = bf16[96,24,128]{2,1,0:T(8,128)(2,1)S(1)} copy-done((bf16[96,24,128]{2,1,0:T(8,128)(2,1)S(1)}, bf16[96,24,128]{2,1,0:T(8,128)(2,1)}, u32[]{:S(2)}) %copy-start.1) | copy-done | bytes 589848
  1.1 0.0 copy-start.2
  1.1 0.9 copy-done.2
  2.0 0.0 copy-start.4
  2.0 0.7 copy-done.4
  2.7 0.0 copy-start.5
  2.7 0.7 copy-done.5
  3.3 0.0 copy-start.6
  3.3 0.7 copy-done.6
  4.0 2.4 %project.1 = (bf16[128,40,128]{2,1,0:T(8,128)(2,1)S(1)}, bf16[2304,128]{1,0:T(8,128)(2,1)S(1)}) custom-call(bf16[2304,128]{1,0:T(8,128)(2,1)S(1)} %bitcast.10, s32[24,96]{1,0:T(8,128)S(1)} %bitcast.11, f32[1,128]{1,0:T(1,128)S(1)} %bitcast.12, f32[1,128]{1,0:T(1,128)S(1)} %bitcast.13, bf16[128,512]{1,0:T(8,128)(2,1)S(1)} %copy-done.2), custom_call_target="tpu_custom_call" | custom-call | tf_op jit(solution)/shard_map/project/pallas_call | solution.py:123
  6.4 51.1 %all_to_all.10.own = bf16[128,40,128]{2,1,0:T(8,128)(2,1)S(1)} all-to-all(bf16[128,40,128]{2,1,0:T(8,128)(2,1)S(1)} %get-tuple-element.7), channel_id=1, replica_groups=mesh['y'=4,'xl'=2,'z'=8,'xh'=2,'core'=2] {'y','xl','z','xh'}, dimensions={0} | all-to-all | bytes 2621440 | tf_op jit(solution)/shard_map/all_to_all | solution.py:141
  57.5 0.0 collective-permute-start
  57.5 3.0 %collective-permute-done.other = bf16[128,40,128]{2,1,0:T(8,128)(2,1)S(1)} collective-permute-done((bf16[128,40,128]{2,1,0:T(8,128)(2,1)S(1)}, bf16[128,40,128]{2,1,0:T(8,128)(2,1)S(1)}, u32[]{:S(2)}, u32[]{:S(2)}) %collective-permute-start) | collective-permute-done | bytes 1310752 | tf_op jit(solution)/shard_map/ppermute | solution.py:142
  60.5 3.5 %product.1 = bf16[128,24,128]{2,1,0:T(8,128)(2,1)} custom-call(s32[1]{0:T(128)} %bitcast.core, bf16[128,40,128]{2,1,0:T(8,128)(2,1)S(1)} %all_to_all.10.own, bf16[128,40,128]{2,1,0:T(8,128)(2,1)S(1)} %collective-permute-done.other), custom_call_target="tpu_custom_call" | custom-call | tf_op jit(solution)/shard_map/product/pallas_call | solution.py:145
  64.1 0.0 copy-start.7
  64.1 0.0 copy-start.8
  64.1 6.9 %all-to-all-start.1 = ((bf16[128,24,128]{2,1,0:T(8,128)(2,1)}), bf16[128,24,128]{2,1,0:T(8,128)(2,1)S(1)}, u32[]{:S(2)}, u32[]{:S(2)}) async-start(bf16[128,24,128]{2,1,0:T(8,128)(2,1)} %product.1), calls=%async_computation.1 | async-start | bytes 1572864 | tf_op jit(solution)/shard_map/all_to_all | solution.py:153
  71.0 0.0 copy-done.7
  71.0 0.1 copy.10.gain
  71.1 0.0 copy-done.8
  71.1 0.1 copy.11.bias
  71.2 0.0 copy-done
  71.2 0.0 copy-start.3
  71.2 0.5 fusion.2.gate
  71.7 24.8 %all-to-all-done.1.tri = bf16[128,24,128]{2,1,0:T(8,128)(2,1)S(1)} async-done(((bf16[128,24,128]{2,1,0:T(8,128)(2,1)}), bf16[128,24,128]{2,1,0:T(8,128)(2,1)S(1)}, u32[]{:S(2)}, u32[]{:S(2)}) %all-to-all-start.1) | async-done | bytes 786464 | tf_op jit(solution)/shard_map/all_to_all | solution.py:153
  96.5 0.0 copy-done.3
  96.5 2.7 %finish.1 = bf16[2304,128]{1,0:T(8,128)(2,1)} custom-call(bf16[128,24,128]{2,1,0:T(8,128)(2,1)S(1)} %all-to-all-done.1.tri, f32[2304,128]{1,0:T(8,128)S(1)} %fusion.2.gate, f32[128,1]{1,0:T(8,128)S(1)} %copy.10.gain, f32[128,1]{1,0:T(8,128)S(1)} %copy.11.bias, bf16[128,128]{1,0:T(8,128)(2,1)S(1)} %copy-done.3), custom_call_target="tpu_custom_call" | custom-call | tf_op jit(solution)/shard_map/finish/pallas_call | solution.py:154
Async XLA Ops:
  0.0 71.2 %copy-start = (bf16[128,128]{1,0:T(8,128)(2,1)S(1)}, bf16[128,128]{1,0:T(8,128)(2,1)}, u32[]{:S(2)}) copy-start(bf16[128,128]{1,0:T(8,128)(2,1)} %param.14) | copy-start | bytes 98308
  0.0 1.1 %copy-start.1 = (bf16[96,24,128]{2,1,0:T(8,128)(2,1)S(1)}, bf16[96,24,128]{2,1,0:T(8,128)(2,1)}, u32[]{:S(2)}) copy-start(bf16[96,24,128]{2,1,0:T(8,128)(2,1)} %param.9) | copy-start | bytes 1769476
  1.1 0.9 copy-start.2
  2.0 0.7 copy-start.4
  2.7 0.7 copy-start.5
  3.3 0.7 copy-start.6
  57.5 3.0 %collective-permute-start = (bf16[128,40,128]{2,1,0:T(8,128)(2,1)S(1)}, bf16[128,40,128]{2,1,0:T(8,128)(2,1)S(1)}, u32[]{:S(2)}, u32[]{:S(2)}) collective-permute-start(bf16[128,40,128]{2,1,0:T(8,128)(2,1)S(1)} %all_to_all.10.own), channel_id=1, source_target_pairs={{0,1},{1,0},{2,3},{3,2},{4,5},{5,4},{6,7},{7,6},{8,9},{9,8},{10,11... | collective-permute-start | bytes 3932168 | tf_op jit(solution)/shard_map/ppermute | solution.py:142
  64.1 6.9 %copy-start.7 = (f32[128]{0:T(128)S(1)}, f32[128]{0:T(128)}, u32[]{:S(2)}) copy-start(f32[128]{0:T(128)} %param.15) | copy-start | bytes 1540
  64.1 7.0 %copy-start.8 = (f32[128]{0:T(128)S(1)}, f32[128]{0:T(128)}, u32[]{:S(2)}) copy-start(f32[128]{0:T(128)} %param.16) | copy-start | bytes 1540
  64.1 32.4 %all-to-all-start.1 = ((bf16[128,24,128]{2,1,0:T(8,128)(2,1)}), bf16[128,24,128]{2,1,0:T(8,128)(2,1)S(1)}, u32[]{:S(2)}, u32[]{:S(2)}) async-start(bf16[128,24,128]{2,1,0:T(8,128)(2,1)} %product.1), calls=%async_computation.1 | async-start | bytes 1572864 | tf_op jit(solution)/shard_map/all_to_all | solution.py:153
  71.2 25.2 %copy-start.3 = (bf16[128,128]{1,0:T(8,128)(2,1)S(1)}, bf16[128,128]{1,0:T(8,128)(2,1)}, u32[]{:S(2)}) copy-start(bf16[128,128]{1,0:T(8,128)(2,1)} %weight.3) | copy-start | bytes 98308

commit v3 on v2

v3 whole, which is shorter than its diff:
```python
import jax
import jax.numpy as jnp
from jax import lax
from jax.experimental import pallas as pl
from jax.experimental.pallas import tpu as pltpu
from jax.sharding import Mesh
from jax.sharding import PartitionSpec as P

CHIPS = ("y", "xl", "z", "xh")
LIMIT = 48 * 1024 * 1024
ROWS = 96
COLS = 24
CH = 128
SENT = 36
BACK = 18
TOKENS = ROWS * COLS
ORDER = ((0, 56, 16), (16, 24, 24), (40, 72, 24), (64, 0, 24), (88, 48, 8), (96, 0, 24), (120, 48, 8))
BF = jnp.bfloat16
F32 = jnp.float32


def dot(a, b, ca, cb):
    return lax.dot_general(a, b, (((ca,), (cb,)), ((), ())), preferred_element_type=F32)


def project_kernel(
    pair, mask, gain, bias, weight, sent, normed, pair_v, mask_v, gain_v, bias_v, weight_v, rows, out, sems
):
    parts = 4
    step = TOKENS // parts
    here = [pl.ds(part * step, step) for part in range(parts)]
    copies = [
        pltpu.make_async_copy(a, b, sems.at[n])
        for n, (a, b) in enumerate(
            [(gain, gain_v), (bias, bias_v)]
            + [(pair.at[h, :], pair_v.at[h, :]) for h in here]
            + [(mask, mask_v), (weight, weight_v)]
        )
    ]
    for copy in copies:
        copy.start()
    copies[0].wait()
    copies[1].wait()
    for part in range(parts):
        copies[2 + part].wait()
        for at in range(part * step, (part + 1) * step, 192):
            x = pair_v[pl.ds(at, 192), :].astype(F32)
            mean = jnp.mean(x, axis=-1, keepdims=True)
            centred = x - mean
            var = jnp.mean(centred * centred, axis=-1, keepdims=True)
            x = (centred * lax.rsqrt(var + 1e-05) * gain_v[...] + bias_v[...]).astype(BF)
            normed[pl.ds(at, 192), :] = x
            rows[pl.ds(at, 192), :] = x.astype(F32)
    copies[-2].wait()
    copies[-1].wait()

    lane = lax.broadcasted_iota(jnp.int32, (ROWS, CH), 1)
    token = lax.broadcasted_iota(jnp.int32, (ROWS, CH), 0)
    source = lane
    for start, first, count in ORDER:
        source = jnp.where((lane >= start) & (lane < start + count), lane - start + first, source)
    spread = (source == token).astype(F32).astype(BF)
    live = dot(mask_v[...].astype(F32).astype(BF), spread, 1, 0)

    turned = weight_v[...].astype(F32).T.astype(BF)
    at_lane = lax.broadcasted_iota(jnp.int32, (CH, CH), 1)

    def column(k):
        x = rows[pl.ds(k, ROWS, stride=COLS), :]
        x = jnp.concatenate([x[first : first + count] for _, first, count in ORDER], axis=0)
        x = x.astype(BF)
        proj = dot(turned, x, 1, 1)
        m = live[k : k + 1, :]
        left = m * jax.nn.sigmoid(proj[:CH]) * proj[CH : 2 * CH]
        right = m * jax.nn.sigmoid(proj[2 * CH : 3 * CH]) * proj[3 * CH :]
        out[pl.ds(k, CH, stride=SENT), :] = jnp.where(at_lane < ROWS, left, right)
        return right

    for k in range(12):
        low = column(k)
        high = column(k + 12)
        out[pl.ds(24 + k, CH, stride=SENT), :] = jnp.where(
            at_lane < 64, low, pltpu.roll(high, 64, 1)
        )
    sent[...] = out[...].astype(BF)


def operands(chunks, wide, shift):
    wide[...] = chunks[...].astype(F32)
    lane = lax.broadcasted_iota(jnp.int32, (384, CH), 1)
    lefts, rights = [], []
    for block in range(8):
        at = block * 16 * SENT
        left = jnp.concatenate(
            [wide[pl.ds(at + k, 16, stride=SENT), :] for k in range(24)], axis=0
        )
        mid = jnp.concatenate(
            [wide[pl.ds(at + 24 + k, 16, stride=SENT), :] for k in range(12)], axis=0
        )
        right = jnp.concatenate([mid, pltpu.roll(mid, 64, 1)], axis=0)
        right = jnp.where(lane < 64, right, left)
        rights.append(pltpu.roll(right, shift, 1))
        lefts.append(left.astype(BF))
    pairs = [
        jnp.where(lane < 64, rights[2 * n], pltpu.roll(rights[2 * n + 1], 64, 1)).astype(BF)
        for n in range(4)
    ]
    return jnp.concatenate(lefts, axis=1), pairs


def product_own_kernel(core, chunks, total, wide):
    left, rights = operands(chunks, wide, jnp.where(core[0] == 0, 32, 112))
    for n in range(4):
        total[pl.ds(n * CH, CH), :] = dot(rights[n].T, left, 1, 0)


def product_other_kernel(core, chunks, total, sent, wide, packed):
    left, rights = operands(chunks, wide, jnp.where(core[0] == 0, 32, 112))
    lane = lax.broadcasted_iota(jnp.int32, (BACK, CH), 1)
    for n in range(4):
        tri = total[pl.ds(n * CH, CH), :] + dot(rights[n].T, left, 1, 0)
        for part, at in enumerate((0, 24, 64, 88)):
            for block in range(8):
                here = tri[at : at + 24, block * CH : (block + 1) * CH]
                tail = here[BACK:]
                tail = jnp.concatenate([pltpu.roll(tail, 96 - 32 * g, 1) for g in range(3)], axis=0)
                packed[pl.ds((block * 16 + n * 4 + part) * BACK, BACK), :] = jnp.where(
                    lane < ROWS, here[:BACK], tail
                )
    sent[...] = packed[...].astype(BF)


def finish_kernel(tri, gate, gain, bias, weight, update, cols, out, done, sems):
    cols[...] = tri[...].astype(F32)
    for row in range(BACK):
        v = cols[pl.ds(row, CH, stride=BACK), :]
        mean = jnp.mean(v, axis=0, keepdims=True)
        centred = v - mean
        var = jnp.mean(centred * centred, axis=0, keepdims=True)
        v = (centred * lax.rsqrt(var + 1e-05) * gain[...] + bias[...]).astype(BF)
        mixed = dot(v, weight[...], 0, 0)
        for start, first, count in ORDER[:5]:
            out[pl.ds(first * COLS + row, count, stride=COLS), :] = mixed[start : start + count]
        group = row // 6
        for start, first, count in ORDER[:5]:
            low, high = max(start, 32 * group), min(start + count, 32 * group + 32)
            if low < high:
                out[pl.ds((first + low - start) * COLS + BACK + row % 6, high - low, stride=COLS), :] = (
                    mixed[ROWS + low - 32 * group : ROWS + high - 32 * group]
                )
    parts = 4
    step = TOKENS // parts
    copies = []
    for part in range(parts):
        here = pl.ds(part * step, step)
        done[here, :] = (gate[here, :] * out[here, :]).astype(BF)
        copies.append(pltpu.make_async_copy(done.at[here, :], update.at[here, :], sems.at[part]))
        copies[-1].start()
    for copy in copies:
        copy.wait()


VMEM = pl.BlockSpec(memory_space=pltpu.VMEM)
SMEM = pl.BlockSpec(memory_space=pltpu.SMEM)
HBM = pl.BlockSpec(memory_space=pltpu.HBM)
PARAMS = pltpu.CompilerParams(vmem_limit_bytes=LIMIT)


def body(
    pair, pair_mask, in_gain, in_bias, input_proj, gate_weight, out_gain, out_bias, out_weight
):
    sent, normed = pl.pallas_call(
        project_kernel,
        out_shape=(
            jax.ShapeDtypeStruct((CH * SENT, CH), BF),
            jax.ShapeDtypeStruct((TOKENS, CH), BF),
        ),
        in_specs=[HBM] * 5,
        out_specs=(VMEM, VMEM),
        scratch_shapes=[
            pltpu.VMEM((TOKENS, CH), BF),
            pltpu.VMEM((COLS, ROWS), jnp.int32),
            pltpu.VMEM((1, CH), F32),
            pltpu.VMEM((1, CH), F32),
            pltpu.VMEM((CH, 4 * CH), BF),
            pltpu.VMEM((TOKENS, CH), F32),
            pltpu.VMEM((CH * SENT, CH), F32),
            pltpu.SemaphoreType.DMA((8,)),
        ],
        compiler_params=pltpu.CompilerParams(vmem_limit_bytes=56 * 1024 * 1024),
        name="project",
    )(
        pair.reshape(TOKENS, CH),
        pair_mask.T,
        in_gain.reshape(1, CH),
        in_bias.reshape(1, CH),
        input_proj,
    )
    own = lax.all_to_all(sent.reshape(CH, 9, 4, CH), CHIPS, 0, 0, tiled=True)
    other = lax.ppermute(own, "core", [(0, 1), (1, 0)])
    gate = jax.nn.sigmoid(jnp.dot(normed, gate_weight, preferred_element_type=F32))
    core = lax.axis_index("core").astype(jnp.int32).reshape(1)
    total = pl.pallas_call(
        product_own_kernel,
        out_shape=jax.ShapeDtypeStruct((4 * CH, 8 * CH), F32),
        in_specs=[SMEM, VMEM],
        out_specs=VMEM,
        scratch_shapes=[pltpu.VMEM((CH * SENT, CH), F32)],
        compiler_params=PARAMS,
        cost_estimate=pl.CostEstimate(flops=4 * 10**8, bytes_accessed=4 * 10**6, transcendentals=0),
        name="product_own",
    )(core, own.reshape(CH * SENT, CH))
    tri = pl.pallas_call(
        product_other_kernel,
        out_shape=jax.ShapeDtypeStruct((CH * BACK, CH), BF),
        in_specs=[SMEM, VMEM, VMEM],
        out_specs=VMEM,
        scratch_shapes=[pltpu.VMEM((CH * SENT, CH), F32), pltpu.VMEM((CH * BACK, CH), F32)],
        compiler_params=PARAMS,
        name="product_other",
    )(core, other.reshape(CH * SENT, CH), total)
    tri = lax.all_to_all(tri.reshape(CH, 9, 2, CH), CHIPS, 0, 0, tiled=True)
    update = pl.pallas_call(
        finish_kernel,
        out_shape=jax.ShapeDtypeStruct((TOKENS, CH), BF),
        in_specs=[VMEM] * 5,
        out_specs=HBM,
        scratch_shapes=[
            pltpu.VMEM((CH * BACK, CH), F32),
            pltpu.VMEM((TOKENS, CH), F32),
            pltpu.VMEM((TOKENS, CH), BF),
            pltpu.SemaphoreType.DMA((4,)),
        ],
        compiler_params=PARAMS,
        name="finish",
    )(tri.reshape(CH * BACK, CH), gate, out_gain.reshape(CH, 1), out_bias.reshape(CH, 1), out_weight)
    return update.reshape(ROWS, COLS, CH)


def solution(mesh):
    fine = Mesh(mesh.devices.reshape(4, 2, 8, 2, 2), ("y", "xl", "z", "xh", "core"))
    split = P(("y", "xl"), ("z", "xh", "core"))
    return jax.shard_map(
        body,
        mesh=fine,
        in_specs=(split, split, P(), P(), P(), P(), P(), P(), P()),
        out_specs=split,
        check_vma=False,
    )
```

time: 99.5 us -> 89.1 us (0.90)
  waiting for transfers between devices: 27.8 us -> 21.7 us
  local copies, waits for them, and re-layouts: 4.23 us -> 0.25 us
  blocking collectives: 51.1 us -> 48.5 us
  Pallas kernels: 8.69 us -> 10.9 us
    all_to_all x1, waiting for transfers between devices: 24.8 us -> 20.5 us  [body(): tri = lax.all_to_all(tri.reshape(CH, 9, 2, CH), CHIPS, 0, 0, tiled=True)]
    unnamed x18 -> x10, local copies, waits for them, and re-layouts: 4.01 us -> 0.02 us
    all_to_all x1, blocking collectives: 51.1 us -> 48.5 us  [body(): own = lax.all_to_all(sent.reshape(CH, 9, 4, CH), CHIPS, 0, 0, tiled=True)]
    pallas_call x3 -> x4, Pallas kernels: 8.69 us -> 10.9 us  [the longest x1 4.46 us: body(): pl.pallas_call(project_kernel, out_shape=(jax.ShapeDtypeStruct((CH * SENT...]
    ppermute x1, waiting for transfers between devices: 3.03 us -> 1.2 us  [body(): other = lax.ppermute(own, 'core', [(0, 1), (1, 0)])]
  transfers between devices with their start and end apart: 2 -> 2, of which waited for: 2 -> 2; matrix products, arithmetic and copies ran while one was open for 1% -> 1% of each run, Pallas kernels for 0% -> 2%
where the time goes in v3:
time: 89.1 us; the launch traced here: 88.8 us
  blocking collectives  48.5 us (54%)
  waiting for transfers between devices  21.7 us (24%)
  Pallas kernels  10.9 us (12%)
  starting transfers between devices  6.91 us (8%)
    all_to_all x1, blocking collectives, body(): own = lax.all_to_all(sent.reshape(CH, 9, 4, CH), CHIPS, 0, 0, tiled=True)  48.5 us
    all_to_all x1, waiting for transfers between devices, body(): tri = lax.all_to_all(tri.reshape(CH, 9, 2, CH), CHIPS, 0, 0, tiled=True)  20.5 us
    all_to_all x1, starting transfers between devices, body(): tri = lax.all_to_all(tri.reshape(CH, 9, 2, CH), CHIPS, 0, 0, tiled=True)  6.91 us
    pallas_call x1, Pallas kernels, body(): pl.pallas_call(project_kernel, out_shape=(jax.ShapeDtypeStruct((CH * SENT...  4.46 us
    pallas_call x1, Pallas kernels, body(): pl.pallas_call(product_other_kernel, out_shape=jax.ShapeDtypeStruct((CH *...  2.56 us
    pallas_call x1, Pallas kernels, body(): pl.pallas_call(finish_kernel, out_shape=jax.ShapeDtypeStruct((TOKENS, CH)...  2.28 us
  transfers between devices with their start and end apart: 2, of which 2 were waited for; matrix products, arithmetic and copies ran while one was open for 1% of the time, Pallas kernels for 2%

profile of v3, /device:TPU:32, one launch (start us, length us, event | category | flops | bytes accessed | tf_op | source)
XLA Modules:
  0.0 88.8 jit_solution(6674615617076506892)
XLA Ops:
  0.0 0.0 copy-start
  0.0 4.5 %project.1 = (bf16[4608,128]{1,0:T(8,128)(2,1)}, bf16[2304,128]{1,0:T(8,128)(2,1)}) custom-call(bf16[2304,128]{1,0:T(8,128)(2,1)} %bitcast.19, s32[24,96]{1,0:T(8,128)} %bitcast.20, f32[1,128]{1,0:T(1,128)} %bitcast.23, f32[1,128]{1,0:T(1,128)} %bitcast.24, bf16[128,512]{1,0:T(8,128)(2,1)} %weight.2), custom_call_target="tpu_custom_call" | custom-call | tf_op jit(solution)/shard_map/project/pallas_call | solution.py:172
  4.5 48.5 %all_to_all.10 = bf16[128,9,4,128]{3,2,1,0:T(4,128)(2,1)S(1)} all-to-all(bf16[128,9,4,128]{3,2,1,0:T(4,128)(2,1)} %bitcast.18), channel_id=1, replica_groups=mesh['y'=4,'xl'=2,'z'=8,'xh'=2,'core'=2] {'y','xl','z','xh'}, dimensions={0} | all-to-all | bytes 2359296 | tf_op jit(solution)/shard_map/all_to_all | solution.py:199
  52.9 0.0 collective-permute-start
  52.9 1.6 %product_own.1.total = f32[512,1024]{1,0:T(8,128)S(1)} custom-call(s32[1]{0:T(128)} %bitcast.core, bf16[4608,128]{1,0:T(8,128)(2,1)S(1)} %bitcast.15), custom_call_target="tpu_custom_call" | custom-call | flops 400000000 | bytes 4000000 | tf_op jit(solution)/shard_map/product_own/pallas_call | solution.py:203
  54.6 1.2 %collective-permute-done = bf16[128,9,4,128]{3,2,1,0:T(4,128)(2,1)S(1)} collective-permute-done((bf16[128,9,4,128]{3,2,1,0:T(4,128)(2,1)S(1)}, bf16[128,9,4,128]{3,2,1,0:T(4,128)(2,1)S(1)}, u32[]{:S(2)}, u32[]{:S(2)}) %collective-permute-start) | collective-permute-done | bytes 1179680 | tf_op jit(solution)/shard_map/ppermute | solution.py:200
  55.8 2.6 %product_other.1 = bf16[2304,128]{1,0:T(8,128)(2,1)} custom-call(s32[1]{0:T(128)} %bitcast.core, bf16[4608,128]{1,0:T(8,128)(2,1)S(1)} %bitcast.17, f32[512,1024]{1,0:T(8,128)S(1)} %product_own.1.total), custom_call_target="tpu_custom_call" | custom-call | tf_op jit(solution)/shard_map/product_other/pallas_call | solution.py:213
  58.3 0.0 copy-start.2
  58.3 0.0 copy-start.3
  58.3 0.0 copy-start.4
  58.3 6.9 %all-to-all-start.1 = ((bf16[128,9,2,128]{3,2,1,0:T(2,128)(2,1)}), bf16[128,9,2,128]{3,2,1,0:T(2,128)(2,1)S(1)}, u32[]{:S(2)}, u32[]{:S(2)}) async-start(bf16[128,9,2,128]{3,2,1,0:T(2,128)(2,1)} %bitcast.8), calls=%async_computation.1 | async-start | bytes 1179648 | tf_op jit(solution)/shard_map/all_to_all | solution.py:222
  65.3 0.0 copy-done.2
  65.3 0.1 copy.10.gain
  65.4 0.0 copy-done.3
  65.4 0.1 copy.11.bias
  65.5 0.0 copy-done
  65.5 0.0 copy-done.4
  65.5 0.0 copy-start.1
  65.5 0.5 fusion.2.gate
  66.0 20.5 %all-to-all-done.1 = bf16[128,9,2,128]{3,2,1,0:T(2,128)(2,1)S(1)} async-done(((bf16[128,9,2,128]{3,2,1,0:T(2,128)(2,1)}), bf16[128,9,2,128]{3,2,1,0:T(2,128)(2,1)S(1)}, u32[]{:S(2)}, u32[]{:S(2)}) %all-to-all-start.1) | async-done | bytes 589856 | tf_op jit(solution)/shard_map/all_to_all | solution.py:222
  86.5 0.0 copy-done.1
  86.5 2.3 %finish.1 = bf16[2304,128]{1,0:T(8,128)(2,1)} custom-call(bf16[2304,128]{1,0:T(8,128)(2,1)S(1)} %bitcast.16, f32[2304,128]{1,0:T(8,128)S(1)} %fusion.2.gate, f32[128,1]{1,0:T(8,128)S(1)} %copy.10.gain, f32[128,1]{1,0:T(8,128)S(1)} %copy.11.bias, bf16[128,128]{1,0:T(8,128)(2,1)S(1)} %copy-done.1), custom_call_target="tpu_custom_call" | custom-call | tf_op jit(solution)/shard_map/finish/pallas_call | solution.py:223
Async XLA Ops:
  0.0 65.5 %copy-start = (bf16[128,128]{1,0:T(8,128)(2,1)S(1)}, bf16[128,128]{1,0:T(8,128)(2,1)}, u32[]{:S(2)}) copy-start(bf16[128,128]{1,0:T(8,128)(2,1)} %param.14) | copy-start | bytes 98308
  52.9 2.8 %collective-permute-start = (bf16[128,9,4,128]{3,2,1,0:T(4,128)(2,1)S(1)}, bf16[128,9,4,128]{3,2,1,0:T(4,128)(2,1)S(1)}, u32[]{:S(2)}, u32[]{:S(2)}) collective-permute-start(bf16[128,9,4,128]{3,2,1,0:T(4,128)(2,1)S(1)} %all_to_all.10), channel_id=1, source_target_pairs={{0,1},{1,0},{2,3},{3,2},{4,5},{5,4},{6,7},{7,6},{8,9},{9,8},{10,11... | collective-permute-start | bytes 3538952 | tf_op jit(solution)/shard_map/ppermute | solution.py:200
  58.3 6.9 %copy-start.2 = (f32[128]{0:T(128)S(1)}, f32[128]{0:T(128)}, u32[]{:S(2)}) copy-start(f32[128]{0:T(128)} %param.15) | copy-start | bytes 1540
  58.3 7.0 %copy-start.3 = (f32[128]{0:T(128)S(1)}, f32[128]{0:T(128)}, u32[]{:S(2)}) copy-start(f32[128]{0:T(128)} %param.16) | copy-start | bytes 1540
  58.3 7.2 %copy-start.4 = (bf16[2304,128]{1,0:T(8,128)(2,1)S(1)}, bf16[2304,128]{1,0:T(8,128)(2,1)}, u32[]{:S(2)}) copy-start(bf16[2304,128]{1,0:T(8,128)(2,1)} %get-tuple-element.8) | copy-start | bytes 1769476
  58.3 28.2 %all-to-all-start.1 = ((bf16[128,9,2,128]{3,2,1,0:T(2,128)(2,1)}), bf16[128,9,2,128]{3,2,1,0:T(2,128)(2,1)S(1)}, u32[]{:S(2)}, u32[]{:S(2)}) async-start(bf16[128,9,2,128]{3,2,1,0:T(2,128)(2,1)} %bitcast.8), calls=%async_computation.1 | async-start | bytes 1179648 | tf_op jit(solution)/shard_map/all_to_all | solution.py:222
  65.5 21.0 %copy-start.1 = (bf16[128,128]{1,0:T(8,128)(2,1)S(1)}, bf16[128,128]{1,0:T(8,128)(2,1)}, u32[]{:S(2)}) copy-start(bf16[128,128]{1,0:T(8,128)(2,1)} %weight.3) | copy-start | bytes 98308

commit v4 on v3

--- a/solution.py
+++ b/solution.py
@@ -21,6 +21,10 @@
 
 def dot(a, b, ca, cb):
     return lax.dot_general(a, b, (((ca,), (cb,)), ((), ())), preferred_element_type=F32)
+
+
+def sigmoid(v):
+    return 0.5 * jnp.tanh(0.5 * v) + 0.5
 
 
 def project_kernel(
@@ -71,8 +75,8 @@
         x = x.astype(BF)
         proj = dot(turned, x, 1, 1)
         m = live[k : k + 1, :]
-        left = m * jax.nn.sigmoid(proj[:CH]) * proj[CH : 2 * CH]
-        right = m * jax.nn.sigmoid(proj[2 * CH : 3 * CH]) * proj[3 * CH :]
+        left = m * sigmoid(proj[:CH]) * proj[CH : 2 * CH]
+        right = m * sigmoid(proj[2 * CH : 3 * CH]) * proj[3 * CH :]
         out[pl.ds(k, CH, stride=SENT), :] = jnp.where(at_lane < ROWS, left, right)
         return right
 
@@ -108,10 +112,18 @@
     return jnp.concatenate(lefts, axis=1), pairs
 
 
-def product_own_kernel(core, chunks, total, wide):
+def product_own_kernel(
+    core, chunks, normed, gate_weight, gain, bias, weight, total, gate, gains, biases, weights, wide
+):
     left, rights = operands(chunks, wide, jnp.where(core[0] == 0, 32, 112))
     for n in range(4):
         total[pl.ds(n * CH, CH), :] = dot(rights[n].T, left, 1, 0)
+    for at in range(0, TOKENS, 256):
+        here = pl.ds(at, 256)
+        gate[here, :] = sigmoid(dot(normed[here, :], gate_weight[...], 1, 0))
+    gains[...] = jnp.broadcast_to(gain[...], (CH, CH)).T
+    biases[...] = jnp.broadcast_to(bias[...], (CH, CH)).T
+    weights[...] = weight[...]
 
 
 def product_other_kernel(core, chunks, total, sent, wide, packed):
@@ -166,14 +178,18 @@
 PARAMS = pltpu.CompilerParams(vmem_limit_bytes=LIMIT)
 
 
+def in_hbm(x):
+    return pltpu.with_memory_space_constraint(x, pltpu.HBM)
+
+
 def body(
     pair, pair_mask, in_gain, in_bias, input_proj, gate_weight, out_gain, out_bias, out_weight
 ):
     sent, normed = pl.pallas_call(
         project_kernel,
         out_shape=(
-            jax.ShapeDtypeStruct((CH * SENT, CH), BF),
-            jax.ShapeDtypeStruct((TOKENS, CH), BF),
+            pltpu.VMEM((CH * SENT, CH), BF),
+            pltpu.VMEM((TOKENS, CH), BF),
         ),
         in_specs=[HBM] * 5,
         out_specs=(VMEM, VMEM),
@@ -187,32 +203,45 @@
             pltpu.VMEM((CH * SENT, CH), F32),
             pltpu.SemaphoreType.DMA((8,)),
         ],
-        compiler_params=pltpu.CompilerParams(vmem_limit_bytes=56 * 1024 * 1024),
+        compiler_params=PARAMS,
         name="project",
     )(
-        pair.reshape(TOKENS, CH),
-        pair_mask.T,
-        in_gain.reshape(1, CH),
-        in_bias.reshape(1, CH),
-        input_proj,
+        in_hbm(pair.reshape(TOKENS, CH)),
+        in_hbm(pair_mask.T),
+        in_hbm(in_gain.reshape(1, CH)),
+        in_hbm(in_bias.reshape(1, CH)),
+        in_hbm(input_proj),
     )
     own = lax.all_to_all(sent.reshape(CH, 9, 4, CH), CHIPS, 0, 0, tiled=True)
     other = lax.ppermute(own, "core", [(0, 1), (1, 0)])
-    gate = jax.nn.sigmoid(jnp.dot(normed, gate_weight, preferred_element_type=F32))
     core = lax.axis_index("core").astype(jnp.int32).reshape(1)
-    total = pl.pallas_call(
+    total, gate, gains, biases, weights = pl.pallas_call(
         product_own_kernel,
-        out_shape=jax.ShapeDtypeStruct((4 * CH, 8 * CH), F32),
-        in_specs=[SMEM, VMEM],
-        out_specs=VMEM,
+        out_shape=(
+            pltpu.VMEM((4 * CH, 8 * CH), F32),
+            pltpu.VMEM((TOKENS, CH), F32),
+            pltpu.VMEM((CH, CH), F32),
+            pltpu.VMEM((CH, CH), F32),
+            pltpu.VMEM((CH, CH), BF),
+        ),
+        in_specs=[SMEM] + [VMEM] * 6,
+        out_specs=[VMEM] * 5,
         scratch_shapes=[pltpu.VMEM((CH * SENT, CH), F32)],
         compiler_params=PARAMS,
         cost_estimate=pl.CostEstimate(flops=4 * 10**8, bytes_accessed=4 * 10**6, transcendentals=0),
         name="product_own",
-    )(core, own.reshape(CH * SENT, CH))
+    )(
+        core,
+        own.reshape(CH * SENT, CH),
+        normed,
+        gate_weight,
+        out_gain.reshape(1, CH),
+        out_bias.reshape(1, CH),
+        out_weight,
+    )
     tri = pl.pallas_call(
         product_other_kernel,
-        out_shape=jax.ShapeDtypeStruct((CH * BACK, CH), BF),
+        out_shape=pltpu.VMEM((CH * BACK, CH), BF),
         in_specs=[SMEM, VMEM, VMEM],
         out_specs=VMEM,
         scratch_shapes=[pltpu.VMEM((CH * SENT, CH), F32), pltpu.VMEM((CH * BACK, CH), F32)],
@@ -233,7 +262,7 @@
         ],
         compiler_params=PARAMS,
         name="finish",
-    )(tri.reshape(CH * BACK, CH), gate, out_gain.reshape(CH, 1), out_bias.reshape(CH, 1), out_weight)
+    )(tri.reshape(CH * BACK, CH), gate, gains, biases, weights)
     return update.reshape(ROWS, COLS, CH)
 
 

time: 89.1 us -> 86.3 us (0.969)
  blocking collectives: 48.5 us -> 76.2 us
  waiting for transfers between devices: 21.7 us -> 1.07 us
  starting transfers between devices: 6.91 us -> 0.01 us
  Pallas kernels: 10.9 us -> 8.69 us
    all_to_all x0 -> x1, blocking collectives: none -> 27.8 us  [body(): tri = lax.all_to_all(tri.reshape(CH, 9, 2, CH), CHIPS, 0, 0, tiled=True)]
    all_to_all x1 -> x0, waiting for transfers between devices: 20.5 us -> none  [body(): tri = lax.all_to_all(tri.reshape(CH, 9, 2, CH), CHIPS, 0, 0, tiled=True)]
    all_to_all x1 -> x0, starting transfers between devices: 6.91 us -> none  [body(): tri = lax.all_to_all(tri.reshape(CH, 9, 2, CH), CHIPS, 0, 0, tiled=True)]
    pallas_call x3, Pallas kernels: 8.66 us -> 7.02 us  [the longest x1 3.54 us: body(): pl.pallas_call(project_kernel, out_shape=(pltpu.VMEM((CH * SENT, CH), BF)...]
  transfers between devices with their start and end apart: 2 -> 1, of which waited for: 2 -> 1; matrix products, arithmetic and copies ran while one was open for 1% -> 0% of each run, Pallas kernels for 2% -> 2%
where the time goes in v4:
time: 86.3 us; the launch traced here: 86.1 us
  blocking collectives  76.2 us (88%)
  Pallas kernels  8.69 us (10%)
  waiting for transfers between devices  1.07 us (1%)
    all_to_all x1, blocking collectives, body(): own = lax.all_to_all(sent.reshape(CH, 9, 4, CH), CHIPS, 0, 0, tiled=True)  48.4 us
    all_to_all x1, blocking collectives, body(): tri = lax.all_to_all(tri.reshape(CH, 9, 2, CH), CHIPS, 0, 0, tiled=True)  27.8 us
    pallas_call x1, Pallas kernels, body(): pl.pallas_call(project_kernel, out_shape=(pltpu.VMEM((CH * SENT, CH), BF)...  3.54 us
    pallas_call x1, Pallas kernels, body(): pl.pallas_call(product_other_kernel, out_shape=pltpu.VMEM((CH * BACK, CH)...  1.74 us
    pallas_call x1, Pallas kernels, body(): pl.pallas_call(product_own_kernel, out_shape=(pltpu.VMEM((4 * CH, 8 * CH)...  1.74 us
  transfers between devices with their start and end apart: 1, of which 1 were waited for; matrix products, arithmetic and copies ran while one was open for 0% of the time, Pallas kernels for 2%

profile of v4, /device:TPU:32, one launch (start us, length us, event | category | flops | bytes accessed | tf_op | source)
XLA Modules:
  0.0 86.1 jit_solution(12520966725783401030)
XLA Ops:
  0.0 3.5 %project.1 = (bf16[4608,128]{1,0:T(8,128)(2,1)S(1)}, bf16[2304,128]{1,0:T(8,128)(2,1)S(1)}) custom-call(bf16[2304,128]{1,0:T(8,128)(2,1)} %bitcast.20, s32[24,96]{1,0:T(8,128)} %bitcast.21, f32[1,128]{1,0:T(1,128)} %bitcast.22, f32[1,128]{1,0:T(1,128)} %bitcast.23, bf16[128,512]{1,0:T(8,128)(2,1)} %weight.2), custom_call_target="tpu_custom_call" | custom-call | tf_op jit(solution)/shard_map/project/pallas_call | solution.py:188
  3.5 0.0 copy-start
  3.6 0.0 copy-start.1
  3.6 0.0 copy-start.2
  3.6 0.0 copy-start.3
  3.6 48.4 %all_to_all.10 = bf16[128,9,4,128]{3,2,1,0:T(4,128)(2,1)S(1)} all-to-all(bf16[128,9,4,128]{3,2,1,0:T(4,128)(2,1)S(1)} %bitcast.16), channel_id=1, replica_groups=mesh['y'=4,'xl'=2,'z'=8,'xh'=2,'core'=2] {'y','xl','z','xh'}, dimensions={0} | all-to-all | bytes 2359296 | tf_op jit(solution)/shard_map/all_to_all | solution.py:215
  52.0 0.0 collective-permute-start
  52.0 0.0 copy-done
  52.0 0.0 copy-done.1
  52.0 0.0 copy-done.2
  52.0 0.0 copy-done.3
  52.0 1.7 %product_own.1 = (f32[512,1024]{1,0:T(8,128)S(1)}, f32[2304,128]{1,0:T(8,128)S(1)}, f32[128,128]{1,0:T(8,128)S(1)}, f32[128,128]{1,0:T(8,128)S(1)}, bf16[128,128]{1,0:T(8,128)(2,1)S(1)}) custom-call(s32[1]{0:T(128)} %bitcast.core, bf16[4608,128]{1,0:T(8,128)(2,1)S(1)} %bitcast.13, bf16[2304,128]{1,0:T(8,128)(2,1)S(1)} %get-tuple-element.13.normed, ...), custom_call_target="tpu_custom_call" | custom-call | flops 400000000 | bytes 4000000 | tf_op jit(solution)/shard_map/product_own/pallas_call | solution.py:218
  53.7 1.1 %collective-permute-done = bf16[128,9,4,128]{3,2,1,0:T(4,128)(2,1)S(1)} collective-permute-done((bf16[128,9,4,128]{3,2,1,0:T(4,128)(2,1)S(1)}, bf16[128,9,4,128]{3,2,1,0:T(4,128)(2,1)S(1)}, u32[]{:S(2)}, u32[]{:S(2)}) %collective-permute-start) | collective-permute-done | bytes 1179680 | tf_op jit(solution)/shard_map/ppermute | solution.py:216
  54.8 1.7 %product_other.1 = bf16[2304,128]{1,0:T(8,128)(2,1)S(1)} custom-call(s32[1]{0:T(128)} %bitcast.core, bf16[4608,128]{1,0:T(8,128)(2,1)S(1)} %bitcast.17, f32[512,1024]{1,0:T(8,128)S(1)} %get-tuple-element.14.total), custom_call_target="tpu_custom_call" | custom-call | tf_op jit(solution)/shard_map/product_other/pallas_call | solution.py:242
  56.6 27.8 %all_to_all.11 = bf16[128,9,2,128]{3,2,1,0:T(2,128)(2,1)S(1)} all-to-all(bf16[128,9,2,128]{3,2,1,0:T(2,128)(2,1)S(1)} %bitcast.15), channel_id=1, replica_groups=mesh['y'=4,'xl'=2,'z'=8,'xh'=2,'core'=2] {'y','xl','z','xh'}, dimensions={0} | all-to-all | bytes 1179648 | tf_op jit(solution)/shard_map/all_to_all | solution.py:251
  84.4 1.7 %finish.1 = bf16[2304,128]{1,0:T(8,128)(2,1)} custom-call(bf16[2304,128]{1,0:T(8,128)(2,1)S(1)} %bitcast.14, f32[2304,128]{1,0:T(8,128)S(1)} %get-tuple-element.15.gate, f32[128,128]{1,0:T(8,128)S(1)} %get-tuple-element.16.gain, f32[128,128]{1,0:T(8,128)S(1)} %get-tuple-element.17.bias, bf16[128,128]{1,0:T(8,128)(2,1)S(1)} %get-tuple-element.18.weight), custom_call_target="tpu_custom_call" | custom-call | tf_op jit(solution)/shard_map/finish/pallas_call | solution.py:252
Async XLA Ops:
  3.5 48.4 %copy-start = (bf16[128,128]{1,0:T(8,128)(2,1)S(1)}, bf16[128,128]{1,0:T(8,128)(2,1)}, u32[]{:S(2)}) copy-start(bf16[128,128]{1,0:T(8,128)(2,1)} %gate_weight.1) | copy-start | bytes 98308
  3.6 48.4 %copy-start.1 = (bf16[128,128]{1,0:T(8,128)(2,1)S(1)}, bf16[128,128]{1,0:T(8,128)(2,1)}, u32[]{:S(2)}) copy-start(bf16[128,128]{1,0:T(8,128)(2,1)} %weight.3) | copy-start | bytes 98308
  3.6 48.4 %copy-start.2 = (f32[128]{0:T(128)S(1)}, f32[128]{0:T(128)}, u32[]{:S(2)}) copy-start(f32[128]{0:T(128)} %param.15) | copy-start | bytes 1540
  3.6 48.4 %copy-start.3 = (f32[128]{0:T(128)S(1)}, f32[128]{0:T(128)}, u32[]{:S(2)}) copy-start(f32[128]{0:T(128)} %param.16) | copy-start | bytes 1540
  52.0 2.8 %collective-permute-start = (bf16[128,9,4,128]{3,2,1,0:T(4,128)(2,1)S(1)}, bf16[128,9,4,128]{3,2,1,0:T(4,128)(2,1)S(1)}, u32[]{:S(2)}, u32[]{:S(2)}) collective-permute-start(bf16[128,9,4,128]{3,2,1,0:T(4,128)(2,1)S(1)} %all_to_all.10), channel_id=1, source_target_pairs={{0,1},{1,0},{2,3},{3,2},{4,5},{5,4},{6,7},{7,6},{8,9},{9,8},{10,11... | collective-permute-start | bytes 3538952 | tf_op jit(solution)/shard_map/ppermute | solution.py:216

commit v5 on v4

--- a/solution.py
+++ b/solution.py
@@ -6,7 +6,7 @@
 from jax.sharding import Mesh
 from jax.sharding import PartitionSpec as P
 
-CHIPS = ("y", "xl", "z", "xh")
+CHIPS = ("xl", "y", "z", "xh")
 LIMIT = 48 * 1024 * 1024
 ROWS = 96
 COLS = 24
@@ -30,23 +30,34 @@
 def project_kernel(
     pair, mask, gain, bias, weight, sent, normed, pair_v, mask_v, gain_v, bias_v, weight_v, rows, out, sems
 ):
-    parts = 4
+    parts = 1
     step = TOKENS // parts
     here = [pl.ds(part * step, step) for part in range(parts)]
     copies = [
         pltpu.make_async_copy(a, b, sems.at[n])
         for n, (a, b) in enumerate(
-            [(gain, gain_v), (bias, bias_v)]
+            [(mask, mask_v), (weight, weight_v), (gain, gain_v), (bias, bias_v)]
             + [(pair.at[h, :], pair_v.at[h, :]) for h in here]
-            + [(mask, mask_v), (weight, weight_v)]
         )
     ]
     for copy in copies:
         copy.start()
+    lane = lax.broadcasted_iota(jnp.int32, (ROWS, CH), 1)
+    token = lax.broadcasted_iota(jnp.int32, (ROWS, CH), 0)
+    source = lane
+    for start, first, count in ORDER:
+        source = jnp.where((lane >= start) & (lane < start + count), lane - start + first, source)
+    spread = (source == token).astype(F32).astype(BF)
     copies[0].wait()
     copies[1].wait()
+    live = dot(mask_v[...].astype(F32).astype(BF), spread, 1, 0)
+    turned = weight_v[...].astype(F32).T.astype(BF)
+    at_lane = lax.broadcasted_iota(jnp.int32, (CH, CH), 1)
+
+    copies[2].wait()
+    copies[3].wait()
     for part in range(parts):
-        copies[2 + part].wait()
+        copies[4 + part].wait()
         for at in range(part * step, (part + 1) * step, 192):
             x = pair_v[pl.ds(at, 192), :].astype(F32)
             mean = jnp.mean(x, axis=-1, keepdims=True)
@@ -55,19 +66,6 @@
             x = (centred * lax.rsqrt(var + 1e-05) * gain_v[...] + bias_v[...]).astype(BF)
             normed[pl.ds(at, 192), :] = x
             rows[pl.ds(at, 192), :] = x.astype(F32)
-    copies[-2].wait()
-    copies[-1].wait()
-
-    lane = lax.broadcasted_iota(jnp.int32, (ROWS, CH), 1)
-    token = lax.broadcasted_iota(jnp.int32, (ROWS, CH), 0)
-    source = lane
-    for start, first, count in ORDER:
-        source = jnp.where((lane >= start) & (lane < start + count), lane - start + first, source)
-    spread = (source == token).astype(F32).astype(BF)
-    live = dot(mask_v[...].astype(F32).astype(BF), spread, 1, 0)
-
-    turned = weight_v[...].astype(F32).T.astype(BF)
-    at_lane = lax.broadcasted_iota(jnp.int32, (CH, CH), 1)
 
     def column(k):
         x = rows[pl.ds(k, ROWS, stride=COLS), :]
@@ -89,18 +87,31 @@
     sent[...] = out[...].astype(BF)
 
 
+SIZES = {"y": 4, "xl": 2, "z": 8, "xh": 2}
+STEP, span = {}, 1
+for axis in reversed(CHIPS):
+    STEP[axis], span = span, span * SIZES[axis]
+
+
+def rank_of(block, z, xh):
+    return block // 2 * STEP["y"] + block % 2 * STEP["xl"] + z * STEP["z"] + xh * STEP["xh"]
+
+
 def operands(chunks, wide, shift):
     wide[...] = chunks[...].astype(F32)
     lane = lax.broadcasted_iota(jnp.int32, (384, CH), 1)
     lefts, rights = [], []
     for block in range(8):
-        at = block * 16 * SENT
-        left = jnp.concatenate(
-            [wide[pl.ds(at + k, 16, stride=SENT), :] for k in range(24)], axis=0
-        )
-        mid = jnp.concatenate(
-            [wide[pl.ds(at + 24 + k, 16, stride=SENT), :] for k in range(12)], axis=0
-        )
+        starts = [rank_of(block, 0, xh) * SENT for xh in range(2)]
+
+        def gather(ks):
+            return jnp.concatenate(
+                [wide[pl.ds(at + k, 8, stride=SENT * STEP["z"]), :] for k in ks for at in starts],
+                axis=0,
+            )
+
+        left = gather(range(24))
+        mid = gather(range(24, SENT))
         right = jnp.concatenate([mid, pltpu.roll(mid, 64, 1)], axis=0)
         right = jnp.where(lane < 64, right, left)
         rights.append(pltpu.roll(right, shift, 1))
@@ -136,7 +147,9 @@
                 here = tri[at : at + 24, block * CH : (block + 1) * CH]
                 tail = here[BACK:]
                 tail = jnp.concatenate([pltpu.roll(tail, 96 - 32 * g, 1) for g in range(3)], axis=0)
-                packed[pl.ds((block * 16 + n * 4 + part) * BACK, BACK), :] = jnp.where(
+                chip = n * 4 + part
+                rank = rank_of(block, chip // 2, chip % 2)
+                packed[pl.ds(rank * BACK, BACK), :] = jnp.where(
                     lane < ROWS, here[:BACK], tail
                 )
     sent[...] = packed[...].astype(BF)

time: 86.3 us -> 85.2 us (0.987)
  blocking collectives: 76.2 us -> 75.2 us
    all_to_all x1, blocking collectives: 48.4 us -> 47 us  [body(): own = lax.all_to_all(sent.reshape(CH, 9, 4, CH), CHIPS, 0, 0, tiled=True)]
where the time goes in v5:
time: 85.2 us; the launch traced here: 84.7 us
  blocking collectives  75.2 us (88%)
  Pallas kernels  8.42 us (10%)
  waiting for transfers between devices  0.92 us (1%)
    all_to_all x1, blocking collectives, body(): own = lax.all_to_all(sent.reshape(CH, 9, 4, CH), CHIPS, 0, 0, tiled=True)  47 us
    all_to_all x1, blocking collectives, body(): tri = lax.all_to_all(tri.reshape(CH, 9, 2, CH), CHIPS, 0, 0, tiled=True)  28.2 us
    pallas_call x1, Pallas kernels, body(): pl.pallas_call(project_kernel, out_shape=(pltpu.VMEM((CH * SENT, CH), BF)...  3.1 us
    pallas_call x1, Pallas kernels, body(): pl.pallas_call(product_own_kernel, out_shape=(pltpu.VMEM((4 * CH, 8 * CH)...  1.89 us
    pallas_call x1, Pallas kernels, body(): pl.pallas_call(product_other_kernel, out_shape=pltpu.VMEM((CH * BACK, CH)...  1.76 us
  transfers between devices with their start and end apart: 1, of which 1 were waited for; matrix products, arithmetic and copies ran while one was open for 0% of the time, Pallas kernels for 2%

profile of v5, /device:TPU:32, one launch (start us, length us, event | category | flops | bytes accessed | tf_op | source)
XLA Modules:
  0.0 84.7 jit_solution(14939866885620553795)
XLA Ops:
  0.0 3.1 %project.1 = (bf16[4608,128]{1,0:T(8,128)(2,1)S(1)}, bf16[2304,128]{1,0:T(8,128)(2,1)S(1)}) custom-call(bf16[2304,128]{1,0:T(8,128)(2,1)} %bitcast.20, s32[24,96]{1,0:T(8,128)} %bitcast.21, f32[1,128]{1,0:T(1,128)} %bitcast.22, f32[1,128]{1,0:T(1,128)} %bitcast.23, bf16[128,512]{1,0:T(8,128)(2,1)} %weight.2), custom_call_target="tpu_custom_call" | custom-call | tf_op jit(solution)/shard_map/project/pallas_call | solution.py:201
  3.1 0.0 copy-start
  3.1 0.0 copy-start.1
  3.1 0.0 copy-start.2
  3.1 0.0 copy-start.3
  3.2 47.0 %all_to_all.10 = bf16[128,9,4,128]{3,2,1,0:T(4,128)(2,1)S(1)} all-to-all(bf16[128,9,4,128]{3,2,1,0:T(4,128)(2,1)S(1)} %bitcast.16), channel_id=1, replica_groups=mesh['y'=4,'xl'=2,'z'=8,'xh'=2,'core'=2] {'xl','y','z','xh'}, dimensions={0} | all-to-all | bytes 2359296 | tf_op jit(solution)/shard_map/all_to_all | solution.py:228
  50.2 0.0 collective-permute-start
  50.2 0.0 copy-done
  50.2 0.0 copy-done.1
  50.2 0.0 copy-done.2
  50.2 0.0 copy-done.3
  50.2 1.9 %product_own.1 = (f32[512,1024]{1,0:T(8,128)S(1)}, f32[2304,128]{1,0:T(8,128)S(1)}, f32[128,128]{1,0:T(8,128)S(1)}, f32[128,128]{1,0:T(8,128)S(1)}, bf16[128,128]{1,0:T(8,128)(2,1)S(1)}) custom-call(s32[1]{0:T(128)} %bitcast.core, bf16[4608,128]{1,0:T(8,128)(2,1)S(1)} %bitcast.13, bf16[2304,128]{1,0:T(8,128)(2,1)S(1)} %get-tuple-element.13.normed, ...), custom_call_target="tpu_custom_call" | custom-call | flops 400000000 | bytes 4000000 | tf_op jit(solution)/shard_map/product_own/pallas_call | solution.py:231
  52.1 0.9 %collective-permute-done = bf16[128,9,4,128]{3,2,1,0:T(4,128)(2,1)S(1)} collective-permute-done((bf16[128,9,4,128]{3,2,1,0:T(4,128)(2,1)S(1)}, bf16[128,9,4,128]{3,2,1,0:T(4,128)(2,1)S(1)}, u32[]{:S(2)}, u32[]{:S(2)}) %collective-permute-start) | collective-permute-done | bytes 1179680 | tf_op jit(solution)/shard_map/ppermute | solution.py:229
  53.0 1.8 %product_other.1 = bf16[2304,128]{1,0:T(8,128)(2,1)S(1)} custom-call(s32[1]{0:T(128)} %bitcast.core, bf16[4608,128]{1,0:T(8,128)(2,1)S(1)} %bitcast.17, f32[512,1024]{1,0:T(8,128)S(1)} %get-tuple-element.14.total), custom_call_target="tpu_custom_call" | custom-call | tf_op jit(solution)/shard_map/product_other/pallas_call | solution.py:255
  54.8 28.2 %all_to_all.11 = bf16[128,9,2,128]{3,2,1,0:T(2,128)(2,1)S(1)} all-to-all(bf16[128,9,2,128]{3,2,1,0:T(2,128)(2,1)S(1)} %bitcast.15), channel_id=1, replica_groups=mesh['y'=4,'xl'=2,'z'=8,'xh'=2,'core'=2] {'xl','y','z','xh'}, dimensions={0} | all-to-all | bytes 1179648 | tf_op jit(solution)/shard_map/all_to_all | solution.py:264
  83.0 1.7 %finish.1 = bf16[2304,128]{1,0:T(8,128)(2,1)} custom-call(bf16[2304,128]{1,0:T(8,128)(2,1)S(1)} %bitcast.14, f32[2304,128]{1,0:T(8,128)S(1)} %get-tuple-element.15.gate, f32[128,128]{1,0:T(8,128)S(1)} %get-tuple-element.16.gain, f32[128,128]{1,0:T(8,128)S(1)} %get-tuple-element.17.bias, bf16[128,128]{1,0:T(8,128)(2,1)S(1)} %get-tuple-element.18.weight), custom_call_target="tpu_custom_call" | custom-call | tf_op jit(solution)/shard_map/finish/pallas_call | solution.py:265
Async XLA Ops:
  3.1 47.1 %copy-start = (bf16[128,128]{1,0:T(8,128)(2,1)S(1)}, bf16[128,128]{1,0:T(8,128)(2,1)}, u32[]{:S(2)}) copy-start(bf16[128,128]{1,0:T(8,128)(2,1)} %gate_weight.1) | copy-start | bytes 98308
  3.1 47.1 %copy-start.1 = (bf16[128,128]{1,0:T(8,128)(2,1)S(1)}, bf16[128,128]{1,0:T(8,128)(2,1)}, u32[]{:S(2)}) copy-start(bf16[128,128]{1,0:T(8,128)(2,1)} %weight.3) | copy-start | bytes 98308
  3.1 47.0 %copy-start.2 = (f32[128]{0:T(128)S(1)}, f32[128]{0:T(128)}, u32[]{:S(2)}) copy-start(f32[128]{0:T(128)} %param.15) | copy-start | bytes 1540
  3.1 47.0 %copy-start.3 = (f32[128]{0:T(128)S(1)}, f32[128]{0:T(128)}, u32[]{:S(2)}) copy-start(f32[128]{0:T(128)} %param.16) | copy-start | bytes 1540
  50.2 2.8 %collective-permute-start = (bf16[128,9,4,128]{3,2,1,0:T(4,128)(2,1)S(1)}, bf16[128,9,4,128]{3,2,1,0:T(4,128)(2,1)S(1)}, u32[]{:S(2)}, u32[]{:S(2)}) collective-permute-start(bf16[128,9,4,128]{3,2,1,0:T(4,128)(2,1)S(1)} %all_to_all.10), channel_id=1, source_target_pairs={{0,1},{1,0},{2,3},{3,2},{4,5},{5,4},{6,7},{7,6},{8,9},{9,8},{10,11... | collective-permute-start | bytes 3538952 | tf_op jit(solution)/shard_map/ppermute | solution.py:229

commit v6 on v5

--- a/solution.py
+++ b/solution.py
@@ -50,8 +50,11 @@
     spread = (source == token).astype(F32).astype(BF)
     copies[0].wait()
     copies[1].wait()
-    live = dot(mask_v[...].astype(F32).astype(BF), spread, 1, 0)
-    turned = weight_v[...].astype(F32).T.astype(BF)
+    half_live = 0.5 * dot(mask_v[...].astype(F32).astype(BF), spread, 1, 0)
+    turned = weight_v[...].astype(F32).T
+    turned = jnp.concatenate(
+        [turned[n * CH : (n + 1) * CH] * (1.0 if n % 2 else 0.5) for n in range(4)], axis=0
+    ).astype(BF)
     at_lane = lax.broadcasted_iota(jnp.int32, (CH, CH), 1)
 
     copies[2].wait()
@@ -63,18 +66,18 @@
             mean = jnp.mean(x, axis=-1, keepdims=True)
             centred = x - mean
             var = jnp.mean(centred * centred, axis=-1, keepdims=True)
-            x = (centred * lax.rsqrt(var + 1e-05) * gain_v[...] + bias_v[...]).astype(BF)
-            normed[pl.ds(at, 192), :] = x
-            rows[pl.ds(at, 192), :] = x.astype(F32)
+            x = centred * lax.rsqrt(var + 1e-05) * gain_v[...] + bias_v[...]
+            normed[pl.ds(at, 192), :] = x.astype(BF)
+            rows[pl.ds(at, 192), :] = x
 
     def column(k):
         x = rows[pl.ds(k, ROWS, stride=COLS), :]
         x = jnp.concatenate([x[first : first + count] for _, first, count in ORDER], axis=0)
         x = x.astype(BF)
         proj = dot(turned, x, 1, 1)
-        m = live[k : k + 1, :]
-        left = m * sigmoid(proj[:CH]) * proj[CH : 2 * CH]
-        right = m * sigmoid(proj[2 * CH : 3 * CH]) * proj[3 * CH :]
+        m = half_live[k : k + 1, :]
+        left = (m * jnp.tanh(proj[:CH]) + m) * proj[CH : 2 * CH]
+        right = (m * jnp.tanh(proj[2 * CH : 3 * CH]) + m) * proj[3 * CH :]
         out[pl.ds(k, CH, stride=SENT), :] = jnp.where(at_lane < ROWS, left, right)
         return right
 
@@ -97,8 +100,9 @@
     return block // 2 * STEP["y"] + block % 2 * STEP["xl"] + z * STEP["z"] + xh * STEP["xh"]
 
 
-def operands(chunks, wide, shift):
+def operands(chunks, wide, core):
     wide[...] = chunks[...].astype(F32)
+    shifts = jnp.where(core == 0, 32, 112), jnp.where(core == 0, 96, 48)
     lane = lax.broadcasted_iota(jnp.int32, (384, CH), 1)
     lefts, rights = [], []
     for block in range(8):
@@ -114,10 +118,10 @@
         mid = gather(range(24, SENT))
         right = jnp.concatenate([mid, pltpu.roll(mid, 64, 1)], axis=0)
         right = jnp.where(lane < 64, right, left)
-        rights.append(pltpu.roll(right, shift, 1))
+        rights.append(pltpu.roll(right, shifts[block % 2], 1))
         lefts.append(left.astype(BF))
     pairs = [
-        jnp.where(lane < 64, rights[2 * n], pltpu.roll(rights[2 * n + 1], 64, 1)).astype(BF)
+        jnp.where(lane < 64, rights[2 * n], rights[2 * n + 1]).astype(BF)
         for n in range(4)
     ]
     return jnp.concatenate(lefts, axis=1), pairs
@@ -126,7 +130,7 @@
 def product_own_kernel(
     core, chunks, normed, gate_weight, gain, bias, weight, total, gate, gains, biases, weights, wide
 ):
-    left, rights = operands(chunks, wide, jnp.where(core[0] == 0, 32, 112))
+    left, rights = operands(chunks, wide, core[0])
     for n in range(4):
         total[pl.ds(n * CH, CH), :] = dot(rights[n].T, left, 1, 0)
     for at in range(0, TOKENS, 256):
@@ -138,7 +142,7 @@
 
 
 def product_other_kernel(core, chunks, total, sent, wide, packed):
-    left, rights = operands(chunks, wide, jnp.where(core[0] == 0, 32, 112))
+    left, rights = operands(chunks, wide, core[0])
     lane = lax.broadcasted_iota(jnp.int32, (BACK, CH), 1)
     for n in range(4):
         tri = total[pl.ds(n * CH, CH), :] + dot(rights[n].T, left, 1, 0)
@@ -152,7 +156,7 @@
                 packed[pl.ds(rank * BACK, BACK), :] = jnp.where(
                     lane < ROWS, here[:BACK], tail
                 )
-    sent[...] = packed[...].astype(BF)
+    sent[...] = packed[pl.ds(0, CH * BACK), :].astype(BF)
 
 
 def finish_kernel(tri, gate, gain, bias, weight, update, cols, out, done, sems):
@@ -257,7 +261,7 @@
         out_shape=pltpu.VMEM((CH * BACK, CH), BF),
         in_specs=[SMEM, VMEM, VMEM],
         out_specs=VMEM,
-        scratch_shapes=[pltpu.VMEM((CH * SENT, CH), F32), pltpu.VMEM((CH * BACK, CH), F32)],
+        scratch_shapes=[pltpu.VMEM((CH * SENT, CH), F32), pltpu.VMEM((CH * BACK + 8, CH), F32)],
         compiler_params=PARAMS,
         name="product_other",
     )(core, other.reshape(CH * SENT, CH), total)

time: 85.2 us -> 84.9 us (level)
  no operation moved by 1% of the time
where the time goes in v6:
time: 84.9 us; the launch traced here: 84.3 us
  blocking collectives  75.2 us (89%)
  Pallas kernels  7.76 us (9%)
  waiting for transfers between devices  1.27 us (1%)
    all_to_all x1, blocking collectives, body(): own = lax.all_to_all(sent.reshape(CH, 9, 4, CH), CHIPS, 0, 0, tiled=True)  47 us
    all_to_all x1, blocking collectives, body(): tri = lax.all_to_all(tri.reshape(CH, 9, 2, CH), CHIPS, 0, 0, tiled=True)  28.2 us
    pallas_call x1, Pallas kernels, body(): pl.pallas_call(project_kernel, out_shape=(pltpu.VMEM((CH * SENT, CH), BF)...  2.93 us
  transfers between devices with their start and end apart: 1, of which 1 were waited for; matrix products, arithmetic and copies ran while one was open for 0% of the time, Pallas kernels for 2%

profile of v6, /device:TPU:32, one launch (start us, length us, event | category | flops | bytes accessed | tf_op | source)
XLA Modules:
  0.0 84.3 jit_solution(1110761642456260548)
XLA Ops:
  0.0 2.9 %project.1 = (bf16[4608,128]{1,0:T(8,128)(2,1)S(1)}, bf16[2304,128]{1,0:T(8,128)(2,1)S(1)}) custom-call(bf16[2304,128]{1,0:T(8,128)(2,1)} %bitcast.20, s32[24,96]{1,0:T(8,128)} %bitcast.21, f32[1,128]{1,0:T(1,128)} %bitcast.22, f32[1,128]{1,0:T(1,128)} %bitcast.23, bf16[128,512]{1,0:T(8,128)(2,1)} %weight.2), custom_call_target="tpu_custom_call" | custom-call | tf_op jit(solution)/shard_map/project/pallas_call | solution.py:205
  2.9 0.0 copy-start
  2.9 0.0 copy-start.1
  3.0 0.0 copy-start.2
  3.0 0.0 copy-start.3
  3.0 47.0 %all_to_all.10 = bf16[128,9,4,128]{3,2,1,0:T(4,128)(2,1)S(1)} all-to-all(bf16[128,9,4,128]{3,2,1,0:T(4,128)(2,1)S(1)} %bitcast.16), channel_id=1, replica_groups=mesh['y'=4,'xl'=2,'z'=8,'xh'=2,'core'=2] {'xl','y','z','xh'}, dimensions={0} | all-to-all | bytes 2359296 | tf_op jit(solution)/shard_map/all_to_all | solution.py:232
  50.0 0.0 collective-permute-start
  50.0 0.0 copy-done
  50.0 0.0 copy-done.1
  50.0 0.0 copy-done.2
  50.0 0.0 copy-done.3
  50.0 1.5 %product_own.1 = (f32[512,1024]{1,0:T(8,128)S(1)}, f32[2304,128]{1,0:T(8,128)S(1)}, f32[128,128]{1,0:T(8,128)S(1)}, f32[128,128]{1,0:T(8,128)S(1)}, bf16[128,128]{1,0:T(8,128)(2,1)S(1)}) custom-call(s32[1]{0:T(128)} %bitcast.core, bf16[4608,128]{1,0:T(8,128)(2,1)S(1)} %bitcast.13, bf16[2304,128]{1,0:T(8,128)(2,1)S(1)} %get-tuple-element.13.normed, ...), custom_call_target="tpu_custom_call" | custom-call | flops 400000000 | bytes 4000000 | tf_op jit(solution)/shard_map/product_own/pallas_call | solution.py:235
  51.6 1.3 %collective-permute-done = bf16[128,9,4,128]{3,2,1,0:T(4,128)(2,1)S(1)} collective-permute-done((bf16[128,9,4,128]{3,2,1,0:T(4,128)(2,1)S(1)}, bf16[128,9,4,128]{3,2,1,0:T(4,128)(2,1)S(1)}, u32[]{:S(2)}, u32[]{:S(2)}) %collective-permute-start) | collective-permute-done | bytes 1179680 | tf_op jit(solution)/shard_map/ppermute | solution.py:233
  52.8 1.6 %product_other.1 = bf16[2304,128]{1,0:T(8,128)(2,1)S(1)} custom-call(s32[1]{0:T(128)} %bitcast.core, bf16[4608,128]{1,0:T(8,128)(2,1)S(1)} %bitcast.17, f32[512,1024]{1,0:T(8,128)S(1)} %get-tuple-element.14.total), custom_call_target="tpu_custom_call" | custom-call | tf_op jit(solution)/shard_map/product_other/pallas_call | solution.py:259
  54.5 28.2 %all_to_all.11 = bf16[128,9,2,128]{3,2,1,0:T(2,128)(2,1)S(1)} all-to-all(bf16[128,9,2,128]{3,2,1,0:T(2,128)(2,1)S(1)} %bitcast.15), channel_id=1, replica_groups=mesh['y'=4,'xl'=2,'z'=8,'xh'=2,'core'=2] {'xl','y','z','xh'}, dimensions={0} | all-to-all | bytes 1179648 | tf_op jit(solution)/shard_map/all_to_all | solution.py:268
  82.7 1.7 %finish.1 = bf16[2304,128]{1,0:T(8,128)(2,1)} custom-call(bf16[2304,128]{1,0:T(8,128)(2,1)S(1)} %bitcast.14, f32[2304,128]{1,0:T(8,128)S(1)} %get-tuple-element.15.gate, f32[128,128]{1,0:T(8,128)S(1)} %get-tuple-element.16.gain, f32[128,128]{1,0:T(8,128)S(1)} %get-tuple-element.17.bias, bf16[128,128]{1,0:T(8,128)(2,1)S(1)} %get-tuple-element.18.weight), custom_call_target="tpu_custom_call" | custom-call | tf_op jit(solution)/shard_map/finish/pallas_call | solution.py:269
Async XLA Ops:
  2.9 47.1 %copy-start = (bf16[128,128]{1,0:T(8,128)(2,1)S(1)}, bf16[128,128]{1,0:T(8,128)(2,1)}, u32[]{:S(2)}) copy-start(bf16[128,128]{1,0:T(8,128)(2,1)} %gate_weight.1) | copy-start | bytes 98308
  2.9 47.0 %copy-start.1 = (bf16[128,128]{1,0:T(8,128)(2,1)S(1)}, bf16[128,128]{1,0:T(8,128)(2,1)}, u32[]{:S(2)}) copy-start(bf16[128,128]{1,0:T(8,128)(2,1)} %weight.3) | copy-start | bytes 98308
  3.0 47.0 %copy-start.2 = (f32[128]{0:T(128)S(1)}, f32[128]{0:T(128)}, u32[]{:S(2)}) copy-start(f32[128]{0:T(128)} %param.15) | copy-start | bytes 1540
  3.0 47.0 %copy-start.3 = (f32[128]{0:T(128)S(1)}, f32[128]{0:T(128)}, u32[]{:S(2)}) copy-start(f32[128]{0:T(128)} %param.16) | copy-start | bytes 1540
  50.0 2.8 %collective-permute-start = (bf16[128,9,4,128]{3,2,1,0:T(4,128)(2,1)S(1)}, bf16[128,9,4,128]{3,2,1,0:T(4,128)(2,1)S(1)}, u32[]{:S(2)}, u32[]{:S(2)}) collective-permute-start(bf16[128,9,4,128]{3,2,1,0:T(4,128)(2,1)S(1)} %all_to_all.10), channel_id=1, source_target_pairs={{0,1},{1,0},{2,3},{3,2},{4,5},{5,4},{6,7},{7,6},{8,9},{9,8},{10,11... | collective-permute-start | bytes 3538952 | tf_op jit(solution)/shard_map/ppermute | solution.py:233

commit v7 on v6

--- a/solution.py
+++ b/solution.py
@@ -6,7 +6,8 @@
 from jax.sharding import Mesh
 from jax.sharding import PartitionSpec as P
 
-CHIPS = ("xl", "y", "z", "xh")
+OUTWARD = ("y", "xl", "z", "xh")
+HOMEWARD = ("xl", "y", "z", "xh")
 LIMIT = 48 * 1024 * 1024
 ROWS = 96
 COLS = 24
@@ -87,30 +88,39 @@
         out[pl.ds(24 + k, CH, stride=SENT), :] = jnp.where(
             at_lane < 64, low, pltpu.roll(high, 64, 1)
         )
-    sent[...] = out[...].astype(BF)
+    sent[...] = out[pl.ds(0, CH * SENT), :].astype(BF)
 
 
 SIZES = {"y": 4, "xl": 2, "z": 8, "xh": 2}
-STEP, span = {}, 1
-for axis in reversed(CHIPS):
-    STEP[axis], span = span, span * SIZES[axis]
-
-
-def rank_of(block, z, xh):
-    return block // 2 * STEP["y"] + block % 2 * STEP["xl"] + z * STEP["z"] + xh * STEP["xh"]
+
+
+def rank_of(order, block, z, xh):
+    rank = 0
+    for axis in order:
+        rank = rank * SIZES[axis] + {"y": block // 2, "xl": block % 2, "z": z, "xh": xh}[axis]
+    return rank
+
+
+STEP = rank_of(OUTWARD, 0, 1, 0)
+
+
+def homeward_rows(values):
+    blocks = sorted(range(8), key=lambda block: rank_of(HOMEWARD, block, 0, 0))
+    starts = [rank_of(OUTWARD, block, 0, 0) for block in blocks]
+    return jnp.concatenate([values[at : at + 16] for at in starts], axis=0)
 
 
 def operands(chunks, wide, core):
-    wide[...] = chunks[...].astype(F32)
+    wide[pl.ds(0, CH * SENT), :] = chunks[...].astype(F32)
     shifts = jnp.where(core == 0, 32, 112), jnp.where(core == 0, 96, 48)
     lane = lax.broadcasted_iota(jnp.int32, (384, CH), 1)
     lefts, rights = [], []
     for block in range(8):
-        starts = [rank_of(block, 0, xh) * SENT for xh in range(2)]
+        starts = [rank_of(OUTWARD, block, 0, xh) * SENT for xh in range(2)]
 
         def gather(ks):
             return jnp.concatenate(
-                [wide[pl.ds(at + k, 8, stride=SENT * STEP["z"]), :] for k in ks for at in starts],
+                [wide[pl.ds(at + k, 8, stride=SENT * STEP), :] for k in ks for at in starts],
                 axis=0,
             )
 
@@ -136,9 +146,9 @@
     for at in range(0, TOKENS, 256):
         here = pl.ds(at, 256)
         gate[here, :] = sigmoid(dot(normed[here, :], gate_weight[...], 1, 0))
-    gains[...] = jnp.broadcast_to(gain[...], (CH, CH)).T
-    biases[...] = jnp.broadcast_to(bias[...], (CH, CH)).T
-    weights[...] = weight[...]
+    gains[...] = homeward_rows(jnp.broadcast_to(gain[...], (CH, CH)).T)
+    biases[...] = homeward_rows(jnp.broadcast_to(bias[...], (CH, CH)).T)
+    weights[...] = homeward_rows(weight[...])
 
 
 def product_other_kernel(core, chunks, total, sent, wide, packed):
@@ -152,7 +162,7 @@
                 tail = here[BACK:]
                 tail = jnp.concatenate([pltpu.roll(tail, 96 - 32 * g, 1) for g in range(3)], axis=0)
                 chip = n * 4 + part
-                rank = rank_of(block, chip // 2, chip % 2)
+                rank = rank_of(HOMEWARD, block, chip // 2, chip % 2)
                 packed[pl.ds(rank * BACK, BACK), :] = jnp.where(
                     lane < ROWS, here[:BACK], tail
                 )
@@ -160,7 +170,7 @@
 
 
 def finish_kernel(tri, gate, gain, bias, weight, update, cols, out, done, sems):
-    cols[...] = tri[...].astype(F32)
+    cols[pl.ds(0, CH * BACK), :] = tri[...].astype(F32)
     for row in range(BACK):
         v = cols[pl.ds(row, CH, stride=BACK), :]
         mean = jnp.mean(v, axis=0, keepdims=True)
@@ -216,8 +226,8 @@
             pltpu.VMEM((1, CH), F32),
             pltpu.VMEM((1, CH), F32),
             pltpu.VMEM((CH, 4 * CH), BF),
-            pltpu.VMEM((TOKENS, CH), F32),
-            pltpu.VMEM((CH * SENT, CH), F32),
+            pltpu.VMEM((TOKENS + COLS, CH), F32),
+            pltpu.VMEM((CH * SENT + SENT, CH), F32),
             pltpu.SemaphoreType.DMA((8,)),
         ],
         compiler_params=PARAMS,
@@ -229,7 +239,7 @@
         in_hbm(in_bias.reshape(1, CH)),
         in_hbm(input_proj),
     )
-    own = lax.all_to_all(sent.reshape(CH, 9, 4, CH), CHIPS, 0, 0, tiled=True)
+    own = lax.all_to_all(sent.reshape(CH, 9, 4, CH), OUTWARD, 0, 0, tiled=True)
     other = lax.ppermute(own, "core", [(0, 1), (1, 0)])
     core = lax.axis_index("core").astype(jnp.int32).reshape(1)
     total, gate, gains, biases, weights = pl.pallas_call(
@@ -243,7 +253,7 @@
         ),
         in_specs=[SMEM] + [VMEM] * 6,
         out_specs=[VMEM] * 5,
-        scratch_shapes=[pltpu.VMEM((CH * SENT, CH), F32)],
+        scratch_shapes=[pltpu.VMEM((CH * SENT + STEP * SENT, CH), F32)],
         compiler_params=PARAMS,
         cost_estimate=pl.CostEstimate(flops=4 * 10**8, bytes_accessed=4 * 10**6, transcendentals=0),
         name="product_own",
@@ -261,19 +271,22 @@
         out_shape=pltpu.VMEM((CH * BACK, CH), BF),
         in_specs=[SMEM, VMEM, VMEM],
         out_specs=VMEM,
-        scratch_shapes=[pltpu.VMEM((CH * SENT, CH), F32), pltpu.VMEM((CH * BACK + 8, CH), F32)],
+        scratch_shapes=[
+            pltpu.VMEM((CH * SENT + STEP * SENT, CH), F32),
+            pltpu.VMEM((CH * BACK + 8, CH), F32),
+        ],
         compiler_params=PARAMS,
         name="product_other",
     )(core, other.reshape(CH * SENT, CH), total)
-    tri = lax.all_to_all(tri.reshape(CH, 9, 2, CH), CHIPS, 0, 0, tiled=True)
+    tri = lax.all_to_all(tri.reshape(CH, 9, 2, CH), HOMEWARD, 0, 0, tiled=True)
     update = pl.pallas_call(
         finish_kernel,
         out_shape=jax.ShapeDtypeStruct((TOKENS, CH), BF),
         in_specs=[VMEM] * 5,
         out_specs=HBM,
         scratch_shapes=[
-            pltpu.VMEM((CH * BACK, CH), F32),
-            pltpu.VMEM((TOKENS, CH), F32),
+            pltpu.VMEM((CH * BACK + BACK, CH), F32),
+            pltpu.VMEM((TOKENS + COLS, CH), F32),
             pltpu.VMEM((TOKENS, CH), BF),
             pltpu.SemaphoreType.DMA((4,)),
         ],

time: 84.9 us -> 84.5 us (level)
  no operation moved by 1% of the time
where the time goes in v7:
time: 84.5 us; the launch traced here: 84 us
  blocking collectives  74.8 us (89%)
  Pallas kernels  7.76 us (9%)
  waiting for transfers between devices  1.27 us (2%)
    all_to_all x1, blocking collectives, body(): own = lax.all_to_all(sent.reshape(CH, 9, 4, CH), OUTWARD, 0, 0, tiled=True)  48.4 us
    all_to_all x1, blocking collectives, body(): tri = lax.all_to_all(tri.reshape(CH, 9, 2, CH), HOMEWARD, 0, 0, tiled=True)  26.5 us
    pallas_call x1, Pallas kernels, body(): pl.pallas_call(project_kernel, out_shape=(pltpu.VMEM((CH * SENT, CH), BF)...  2.93 us
  transfers between devices with their start and end apart: 1, of which 1 were waited for; matrix products, arithmetic and copies ran while one was open for 0% of the time, Pallas kernels for 2%

profile of v7, /device:TPU:32, one launch (start us, length us, event | category | flops | bytes accessed | tf_op | source)
XLA Modules:
  0.0 84.0 jit_solution(11344262406608741231)
XLA Ops:
  0.0 2.9 %project.1 = (bf16[4608,128]{1,0:T(8,128)(2,1)S(1)}, bf16[2304,128]{1,0:T(8,128)(2,1)S(1)}) custom-call(bf16[2304,128]{1,0:T(8,128)(2,1)} %bitcast.20, s32[24,96]{1,0:T(8,128)} %bitcast.21, f32[1,128]{1,0:T(1,128)} %bitcast.22, f32[1,128]{1,0:T(1,128)} %bitcast.23, bf16[128,512]{1,0:T(8,128)(2,1)} %weight.2), custom_call_target="tpu_custom_call" | custom-call | tf_op jit(solution)/shard_map/project/pallas_call | solution.py:215
  2.9 0.0 copy-start
  2.9 0.0 copy-start.1
  3.0 0.0 copy-start.2
  3.0 0.0 copy-start.3
  3.0 48.4 %all_to_all.10 = bf16[128,9,4,128]{3,2,1,0:T(4,128)(2,1)S(1)} all-to-all(bf16[128,9,4,128]{3,2,1,0:T(4,128)(2,1)S(1)} %bitcast.16), channel_id=1, replica_groups=mesh['y'=4,'xl'=2,'z'=8,'xh'=2,'core'=2] {'y','xl','z','xh'}, dimensions={0} | all-to-all | bytes 2359296 | tf_op jit(solution)/shard_map/all_to_all | solution.py:242
  51.4 0.0 collective-permute-start
  51.4 0.0 copy-done
  51.4 0.0 copy-done.1
  51.4 0.0 copy-done.2
  51.4 0.0 copy-done.3
  51.4 1.5 %product_own.1 = (f32[512,1024]{1,0:T(8,128)S(1)}, f32[2304,128]{1,0:T(8,128)S(1)}, f32[128,128]{1,0:T(8,128)S(1)}, f32[128,128]{1,0:T(8,128)S(1)}, bf16[128,128]{1,0:T(8,128)(2,1)S(1)}) custom-call(s32[1]{0:T(128)} %bitcast.core, bf16[4608,128]{1,0:T(8,128)(2,1)S(1)} %bitcast.13, bf16[2304,128]{1,0:T(8,128)(2,1)S(1)} %get-tuple-element.13.normed, ...), custom_call_target="tpu_custom_call" | custom-call | flops 400000000 | bytes 4000000 | tf_op jit(solution)/shard_map/product_own/pallas_call | solution.py:245
  52.9 1.3 %collective-permute-done = bf16[128,9,4,128]{3,2,1,0:T(4,128)(2,1)S(1)} collective-permute-done((bf16[128,9,4,128]{3,2,1,0:T(4,128)(2,1)S(1)}, bf16[128,9,4,128]{3,2,1,0:T(4,128)(2,1)S(1)}, u32[]{:S(2)}, u32[]{:S(2)}) %collective-permute-start) | collective-permute-done | bytes 1179680 | tf_op jit(solution)/shard_map/ppermute | solution.py:243
  54.2 1.6 %product_other.1 = bf16[2304,128]{1,0:T(8,128)(2,1)S(1)} custom-call(s32[1]{0:T(128)} %bitcast.core, bf16[4608,128]{1,0:T(8,128)(2,1)S(1)} %bitcast.17, f32[512,1024]{1,0:T(8,128)S(1)} %get-tuple-element.14.total), custom_call_target="tpu_custom_call" | custom-call | tf_op jit(solution)/shard_map/product_other/pallas_call | solution.py:269
  55.8 26.5 %all_to_all.11 = bf16[128,9,2,128]{3,2,1,0:T(2,128)(2,1)S(1)} all-to-all(bf16[128,9,2,128]{3,2,1,0:T(2,128)(2,1)S(1)} %bitcast.15), channel_id=1, replica_groups=mesh['y'=4,'xl'=2,'z'=8,'xh'=2,'core'=2] {'xl','y','z','xh'}, dimensions={0} | all-to-all | bytes 1179648 | tf_op jit(solution)/shard_map/all_to_all | solution.py:281
  82.3 1.7 %finish.1 = bf16[2304,128]{1,0:T(8,128)(2,1)} custom-call(bf16[2304,128]{1,0:T(8,128)(2,1)S(1)} %bitcast.14, f32[2304,128]{1,0:T(8,128)S(1)} %get-tuple-element.15.gate, f32[128,128]{1,0:T(8,128)S(1)} %get-tuple-element.16.gain, f32[128,128]{1,0:T(8,128)S(1)} %get-tuple-element.17.bias, bf16[128,128]{1,0:T(8,128)(2,1)S(1)} %get-tuple-element.18.weight), custom_call_target="tpu_custom_call" | custom-call | tf_op jit(solution)/shard_map/finish/pallas_call | solution.py:282
Async XLA Ops:
  2.9 48.4 %copy-start = (bf16[128,128]{1,0:T(8,128)(2,1)S(1)}, bf16[128,128]{1,0:T(8,128)(2,1)}, u32[]{:S(2)}) copy-start(bf16[128,128]{1,0:T(8,128)(2,1)} %gate_weight.1) | copy-start | bytes 98308
  2.9 48.4 %copy-start.1 = (bf16[128,128]{1,0:T(8,128)(2,1)S(1)}, bf16[128,128]{1,0:T(8,128)(2,1)}, u32[]{:S(2)}) copy-start(bf16[128,128]{1,0:T(8,128)(2,1)} %weight.3) | copy-start | bytes 98308
  3.0 48.4 %copy-start.2 = (f32[128]{0:T(128)S(1)}, f32[128]{0:T(128)}, u32[]{:S(2)}) copy-start(f32[128]{0:T(128)} %param.15) | copy-start | bytes 1540
  3.0 48.4 %copy-start.3 = (f32[128]{0:T(128)S(1)}, f32[128]{0:T(128)}, u32[]{:S(2)}) copy-start(f32[128]{0:T(128)} %param.16) | copy-start | bytes 1540
  51.4 2.8 %collective-permute-start = (bf16[128,9,4,128]{3,2,1,0:T(4,128)(2,1)S(1)}, bf16[128,9,4,128]{3,2,1,0:T(4,128)(2,1)S(1)}, u32[]{:S(2)}, u32[]{:S(2)}) collective-permute-start(bf16[128,9,4,128]{3,2,1,0:T(4,128)(2,1)S(1)} %all_to_all.10), channel_id=1, source_target_pairs={{0,1},{1,0},{2,3},{3,2},{4,5},{5,4},{6,7},{7,6},{8,9},{9,8},{10,11... | collective-permute-start | bytes 3538952 | tf_op jit(solution)/shard_map/ppermute | solution.py:243

commit v8 on v7

--- a/solution.py
+++ b/solution.py
@@ -110,13 +110,14 @@
     return jnp.concatenate([values[at : at + 16] for at in starts], axis=0)
 
 
-def operands(chunks, wide, core):
-    wide[pl.ds(0, CH * SENT), :] = chunks[...].astype(F32)
+def operands(chunks, wide, core, blocks=range(8)):
+    base = rank_of(OUTWARD, blocks[0], 0, 0)
+    wide[pl.ds(0, len(blocks) * 16 * SENT), :] = chunks[...].astype(F32)
     shifts = jnp.where(core == 0, 32, 112), jnp.where(core == 0, 96, 48)
     lane = lax.broadcasted_iota(jnp.int32, (384, CH), 1)
     lefts, rights = [], []
-    for block in range(8):
-        starts = [rank_of(OUTWARD, block, 0, xh) * SENT for xh in range(2)]
+    for block in blocks:
+        starts = [(rank_of(OUTWARD, block, 0, xh) - base) * SENT for xh in range(2)]
 
         def gather(ks):
             return jnp.concatenate(
@@ -132,7 +133,7 @@
         lefts.append(left.astype(BF))
     pairs = [
         jnp.where(lane < 64, rights[2 * n], rights[2 * n + 1]).astype(BF)
-        for n in range(4)
+        for n in range(len(blocks) // 2)
     ]
     return jnp.concatenate(lefts, axis=1), pairs
 
@@ -151,8 +152,17 @@
     weights[...] = homeward_rows(weight[...])
 
 
-def product_other_kernel(core, chunks, total, sent, wide, packed):
-    left, rights = operands(chunks, wide, core[0])
+def prepare_kernel(core, chunks, left, right, wide):
+    lefts, rights = operands(chunks, wide, core[0], range(4))
+    left[...] = lefts
+    for n in range(2):
+        right[n] = rights[n]
+
+
+def product_other_kernel(core, chunks, left_first, right_first, total, sent, wide, packed):
+    left, rights = operands(chunks, wide, core[0], range(4, 8))
+    left = jnp.concatenate([left_first[...], left], axis=1)
+    rights = [right_first[0], right_first[1]] + rights
     lane = lax.broadcasted_iota(jnp.int32, (BACK, CH), 1)
     for n in range(4):
         tri = total[pl.ds(n * CH, CH), :] + dot(rights[n].T, left, 1, 0)
@@ -240,7 +250,9 @@
         in_hbm(input_proj),
     )
     own = lax.all_to_all(sent.reshape(CH, 9, 4, CH), OUTWARD, 0, 0, tiled=True)
-    other = lax.ppermute(own, "core", [(0, 1), (1, 0)])
+    swap = [(0, 1), (1, 0)]
+    other_first = lax.ppermute(own[: CH // 2], "core", swap)
+    other_last = lax.ppermute(own[CH // 2 :], "core", swap)
     core = lax.axis_index("core").astype(jnp.int32).reshape(1)
     total, gate, gains, biases, weights = pl.pallas_call(
         product_own_kernel,
@@ -266,18 +278,29 @@
         out_bias.reshape(1, CH),
         out_weight,
     )
+    half = CH // 2 * SENT
+    left_first, right_first = pl.pallas_call(
+        prepare_kernel,
+        out_shape=(pltpu.VMEM((384, 4 * CH), BF), pltpu.VMEM((2, 384, CH), BF)),
+        in_specs=[SMEM, VMEM],
+        out_specs=[VMEM] * 2,
+        scratch_shapes=[pltpu.VMEM((half + STEP * SENT, CH), F32)],
+        compiler_params=PARAMS,
+        cost_estimate=pl.CostEstimate(flops=10**8, bytes_accessed=2 * 10**6, transcendentals=0),
+        name="prepare",
+    )(core, other_first.reshape(half, CH))
     tri = pl.pallas_call(
         product_other_kernel,
         out_shape=pltpu.VMEM((CH * BACK, CH), BF),
-        in_specs=[SMEM, VMEM, VMEM],
+        in_specs=[SMEM] + [VMEM] * 4,
         out_specs=VMEM,
         scratch_shapes=[
-            pltpu.VMEM((CH * SENT + STEP * SENT, CH), F32),
+            pltpu.VMEM((half + STEP * SENT, CH), F32),
             pltpu.VMEM((CH * BACK + 8, CH), F32),
         ],
         compiler_params=PARAMS,
         name="product_other",
-    )(core, other.reshape(CH * SENT, CH), total)
+    )(core, other_last.reshape(half, CH), left_first, right_first, total)
     tri = lax.all_to_all(tri.reshape(CH, 9, 2, CH), HOMEWARD, 0, 0, tiled=True)
     update = pl.pallas_call(
         finish_kernel,

time: 84.5 us -> 85.7 us (1.014)
  local copies, waits for them, and re-layouts: 0.03 us -> 1.43 us
    slice x0 -> x1, local copies, waits for them, and re-layouts: none -> 1.42 us  [body(): other_first = lax.ppermute(own[:CH // 2], 'core', swap)]
  transfers between devices with their start and end apart: 1 -> 2, of which waited for: 1 -> 2; matrix products, arithmetic and copies ran while one was open for 0% -> 0% of each run, Pallas kernels for 2% -> 2%
where the time goes in v8:
time: 85.7 us; the launch traced here: 85.1 us
  blocking collectives  74.7 us (87%)
  Pallas kernels  7.88 us (9%)
  local copies, waits for them, and re-layouts  1.43 us (2%)
    all_to_all x1, blocking collectives, body(): own = lax.all_to_all(sent.reshape(CH, 9, 4, CH), OUTWARD, 0, 0, tiled=True)  48.2 us
    all_to_all x1, blocking collectives, body(): tri = lax.all_to_all(tri.reshape(CH, 9, 2, CH), HOMEWARD, 0, 0, tiled=True)  26.5 us
    pallas_call x1, Pallas kernels, body(): pl.pallas_call(project_kernel, out_shape=(pltpu.VMEM((CH * SENT, CH), BF)...  2.93 us
  transfers between devices with their start and end apart: 2, of which 2 were waited for; matrix products, arithmetic and copies ran while one was open for 0% of the time, Pallas kernels for 2%

profile of v8, /device:TPU:32, one launch (start us, length us, event | category | flops | bytes accessed | tf_op | source)
XLA Modules:
  0.0 85.1 jit_solution(15519803651140251580)
XLA Ops:
  0.0 2.9 %project.1 = (bf16[4608,128]{1,0:T(8,128)(2,1)S(1)}, bf16[2304,128]{1,0:T(8,128)(2,1)S(1)}) custom-call(bf16[2304,128]{1,0:T(8,128)(2,1)} %bitcast.22, s32[24,96]{1,0:T(8,128)} %bitcast.23, f32[1,128]{1,0:T(1,128)} %bitcast.24, f32[1,128]{1,0:T(1,128)} %bitcast.25, bf16[128,512]{1,0:T(8,128)(2,1)} %weight.2), custom_call_target="tpu_custom_call" | custom-call | tf_op jit(solution)/shard_map/project/pallas_call | solution.py:225
  2.9 48.2 %all_to_all.10 = bf16[128,9,4,128]{3,2,1,0:T(4,128)(2,1)S(1)} all-to-all(bf16[128,9,4,128]{3,2,1,0:T(4,128)(2,1)S(1)} %bitcast.17), channel_id=1, replica_groups=mesh['y'=4,'xl'=2,'z'=8,'xh'=2,'core'=2] {'y','xl','z','xh'}, dimensions={0} | all-to-all | bytes 2359296 | tf_op jit(solution)/shard_map/all_to_all | solution.py:252
  51.2 0.0 copy-start
  51.2 0.0 copy-start.1
  51.2 0.0 copy-start.2
  51.2 0.0 copy-start.3
  51.2 1.4 %fusion = (bf16[64,9,4,128]{3,2,1,0:T(4,128)(2,1)}, bf16[64,9,4,128]{3,2,1,0:T(4,128)(2,1)}) fusion(bf16[128,9,4,128]{3,2,1,0:T(4,128)(2,1)S(1)} %all_to_all.10), kind=kLoop, calls=%fused_computation | loop fusion | bytes 2359296 | tf_op jit(solution)/shard_map/slice | solution.py:254
  52.6 0.0 collective-permute-start.1
  52.6 0.5 collective-permute-start
  53.1 0.0 copy-done
  53.1 0.0 copy-done.1
  53.1 0.0 copy-done.2
  53.1 0.0 copy-done.3
  53.1 1.5 %product_own.1 = (f32[512,1024]{1,0:T(8,128)S(1)}, f32[2304,128]{1,0:T(8,128)S(1)}, f32[128,128]{1,0:T(8,128)S(1)}, f32[128,128]{1,0:T(8,128)S(1)}, bf16[128,128]{1,0:T(8,128)(2,1)S(1)}) custom-call(s32[1]{0:T(128)} %bitcast.core, bf16[4608,128]{1,0:T(8,128)(2,1)S(1)} %bitcast.14, bf16[2304,128]{1,0:T(8,128)(2,1)S(1)} %get-tuple-element.17.normed, ...), custom_call_target="tpu_custom_call" | custom-call | flops 400000000 | bytes 4000000 | tf_op jit(solution)/shard_map/product_own/pallas_call | solution.py:257
  54.7 0.1 collective-permute-done.1
  54.8 0.4 prepare.1
  55.2 0.4 collective-permute-done
  55.7 1.3 %product_other.1 = bf16[2304,128]{1,0:T(8,128)(2,1)S(1)} custom-call(s32[1]{0:T(128)} %bitcast.core, bf16[2304,128]{1,0:T(8,128)(2,1)S(1)} %bitcast.19, bf16[384,512]{1,0:T(8,128)(2,1)S(1)} %get-tuple-element.15.left_first, bf16[2,384,128]{2,1,0:T(8,128)(2,1)S(1)} %get-tuple-element.16.right_first, f32[512,1024]{1,0:T(8,128)S(1)} %get-tuple-element.18.total), custom_call_target="tpu_custom_call" | custom-call | tf_op jit(solution)/shard_map/product_other/pallas_call | solution.py:292
  57.0 26.5 %all_to_all.11 = bf16[128,9,2,128]{3,2,1,0:T(2,128)(2,1)S(1)} all-to-all(bf16[128,9,2,128]{3,2,1,0:T(2,128)(2,1)S(1)} %bitcast.16), channel_id=1, replica_groups=mesh['y'=4,'xl'=2,'z'=8,'xh'=2,'core'=2] {'xl','y','z','xh'}, dimensions={0} | all-to-all | bytes 1179648 | tf_op jit(solution)/shard_map/all_to_all | solution.py:304
  83.5 1.7 %finish.1 = bf16[2304,128]{1,0:T(8,128)(2,1)} custom-call(bf16[2304,128]{1,0:T(8,128)(2,1)S(1)} %bitcast.15, f32[2304,128]{1,0:T(8,128)S(1)} %get-tuple-element.19.gate, f32[128,128]{1,0:T(8,128)S(1)} %get-tuple-element.20.gain, f32[128,128]{1,0:T(8,128)S(1)} %get-tuple-element.21.bias, bf16[128,128]{1,0:T(8,128)(2,1)S(1)} %get-tuple-element.22.weight), custom_call_target="tpu_custom_call" | custom-call | tf_op jit(solution)/shard_map/finish/pallas_call | solution.py:305
Async XLA Ops:
  51.2 1.9 %copy-start = (bf16[128,128]{1,0:T(8,128)(2,1)S(1)}, bf16[128,128]{1,0:T(8,128)(2,1)}, u32[]{:S(2)}) copy-start(bf16[128,128]{1,0:T(8,128)(2,1)} %gate_weight.1) | copy-start | bytes 98308
  51.2 1.9 %copy-start.1 = (bf16[128,128]{1,0:T(8,128)(2,1)S(1)}, bf16[128,128]{1,0:T(8,128)(2,1)}, u32[]{:S(2)}) copy-start(bf16[128,128]{1,0:T(8,128)(2,1)} %weight.3) | copy-start | bytes 98308
  51.2 1.9 %copy-start.2 = (f32[128]{0:T(128)S(1)}, f32[128]{0:T(128)}, u32[]{:S(2)}) copy-start(f32[128]{0:T(128)} %param.15) | copy-start | bytes 1540
  51.2 1.9 %copy-start.3 = (f32[128]{0:T(128)S(1)}, f32[128]{0:T(128)}, u32[]{:S(2)}) copy-start(f32[128]{0:T(128)} %param.16) | copy-start | bytes 1540
  52.6 2.2 %collective-permute-start.1 = (bf16[64,9,4,128]{3,2,1,0:T(4,128)(2,1)}, bf16[64,9,4,128]{3,2,1,0:T(4,128)(2,1)S(1)}, u32[]{:S(2)}, u32[]{:S(2)}) collective-permute-start(bf16[64,9,4,128]{3,2,1,0:T(4,128)(2,1)} %get-tuple-element.23), channel_id=1, source_target_pairs={{0,1},{1,0},{2,3},{3,2},{4,5},{5,4},{6,7},{7,6},{8,9},{9,8},{10,11... | collective-permute-start | bytes 1769480 | tf_op jit(solution)/shard_map/ppermute | solution.py:254
  52.6 3.1 %collective-permute-start = (bf16[64,9,4,128]{3,2,1,0:T(4,128)(2,1)}, bf16[64,9,4,128]{3,2,1,0:T(4,128)(2,1)S(1)}, u32[]{:S(2)}, u32[]{:S(2)}) collective-permute-start(bf16[64,9,4,128]{3,2,1,0:T(4,128)(2,1)} %get-tuple-element.24), channel_id=1, source_target_pairs={{0,1},{1,0},{2,3},{3,2},{4,5},{5,4},{6,7},{7,6},{8,9},{9,8},{10,11... | collective-permute-start | bytes 1769480 | tf_op jit(solution)/shard_map/ppermute | solution.py:255

commit v9 on v7

--- a/solution.py
+++ b/solution.py
@@ -29,7 +29,7 @@
 
 
 def project_kernel(
-    pair, mask, gain, bias, weight, sent, normed, pair_v, mask_v, gain_v, bias_v, weight_v, rows, out, sems
+    pair, mask, gain, bias, weight, sent, pair_v, mask_v, gain_v, bias_v, weight_v, rows, out, sems
 ):
     parts = 1
     step = TOKENS // parts
@@ -68,7 +68,6 @@
             centred = x - mean
             var = jnp.mean(centred * centred, axis=-1, keepdims=True)
             x = centred * lax.rsqrt(var + 1e-05) * gain_v[...] + bias_v[...]
-            normed[pl.ds(at, 192), :] = x.astype(BF)
             rows[pl.ds(at, 192), :] = x
 
     def column(k):
@@ -138,14 +137,18 @@
 
 
 def product_own_kernel(
-    core, chunks, normed, gate_weight, gain, bias, weight, total, gate, gains, biases, weights, wide
+    core, chunks, pair, in_gain, in_bias, gate_weight, gain, bias, weight, total, gate, gains, biases, weights, wide
 ):
     left, rights = operands(chunks, wide, core[0])
     for n in range(4):
         total[pl.ds(n * CH, CH), :] = dot(rights[n].T, left, 1, 0)
     for at in range(0, TOKENS, 256):
         here = pl.ds(at, 256)
-        gate[here, :] = sigmoid(dot(normed[here, :], gate_weight[...], 1, 0))
+        x = pair[here, :].astype(F32)
+        centred = x - jnp.mean(x, axis=-1, keepdims=True)
+        var = jnp.mean(centred * centred, axis=-1, keepdims=True)
+        x = centred * lax.rsqrt(var + 1e-05) * in_gain[...] + in_bias[...]
+        gate[here, :] = sigmoid(dot(x.astype(BF), gate_weight[...], 1, 0))
     gains[...] = homeward_rows(jnp.broadcast_to(gain[...], (CH, CH)).T)
     biases[...] = homeward_rows(jnp.broadcast_to(bias[...], (CH, CH)).T)
     weights[...] = homeward_rows(weight[...])
@@ -212,14 +215,11 @@
 def body(
     pair, pair_mask, in_gain, in_bias, input_proj, gate_weight, out_gain, out_bias, out_weight
 ):
-    sent, normed = pl.pallas_call(
+    sent = pl.pallas_call(
         project_kernel,
-        out_shape=(
-            pltpu.VMEM((CH * SENT, CH), BF),
-            pltpu.VMEM((TOKENS, CH), BF),
-        ),
+        out_shape=pltpu.VMEM((CH * SENT, CH), BF),
         in_specs=[HBM] * 5,
-        out_specs=(VMEM, VMEM),
+        out_specs=VMEM,
         scratch_shapes=[
             pltpu.VMEM((TOKENS, CH), BF),
             pltpu.VMEM((COLS, ROWS), jnp.int32),
@@ -251,7 +251,7 @@
             pltpu.VMEM((CH, CH), F32),
             pltpu.VMEM((CH, CH), BF),
         ),
-        in_specs=[SMEM] + [VMEM] * 6,
+        in_specs=[SMEM] + [VMEM] * 8,
         out_specs=[VMEM] * 5,
         scratch_shapes=[pltpu.VMEM((CH * SENT + STEP * SENT, CH), F32)],
         compiler_params=PARAMS,
@@ -260,7 +260,9 @@
     )(
         core,
         own.reshape(CH * SENT, CH),
-        normed,
+        pair.reshape(TOKENS, CH),
+        in_gain.reshape(1, CH),
+        in_bias.reshape(1, CH),
         gate_weight,
         out_gain.reshape(1, CH),
         out_bias.reshape(1, CH),

time: 84.5 us -> 84.6 us (level)
  no operation moved by 1% of the time
where the time goes in v9:
time: 84.6 us; the launch traced here: 84 us
  blocking collectives  74.8 us (88%)
  Pallas kernels  8.16 us (10%)
    all_to_all x1, blocking collectives, body(): own = lax.all_to_all(sent.reshape(CH, 9, 4, CH), OUTWARD, 0, 0, tiled=True)  48.4 us
    all_to_all x1, blocking collectives, body(): tri = lax.all_to_all(tri.reshape(CH, 9, 2, CH), HOMEWARD, 0, 0, tiled=True)  26.4 us
    pallas_call x1, Pallas kernels, body(): pl.pallas_call(project_kernel, out_shape=pltpu.VMEM((CH * SENT, CH), BF),...  2.92 us
    pallas_call x1, Pallas kernels, body(): pl.pallas_call(product_own_kernel, out_shape=(pltpu.VMEM((4 * CH, 8 * CH)...  1.94 us
  transfers between devices with their start and end apart: 1, of which 1 were waited for; matrix products, arithmetic and copies ran while one was open for 0% of the time, Pallas kernels for 2%

profile of v9, /device:TPU:32, one launch (start us, length us, event | category | flops | bytes accessed | tf_op | source)
XLA Modules:
  0.0 84.0 jit_solution(1545604252159974757)
XLA Ops:
  0.0 2.9 %project.1 = bf16[4608,128]{1,0:T(8,128)(2,1)S(1)} custom-call(bf16[2304,128]{1,0:T(8,128)(2,1)} %bitcast.15, s32[24,96]{1,0:T(8,128)} %bitcast.26, f32[1,128]{1,0:T(1,128)} %bitcast.20, f32[1,128]{1,0:T(1,128)} %bitcast.22, bf16[128,512]{1,0:T(8,128)(2,1)} %weight.2), custom_call_target="tpu_custom_call" | custom-call | tf_op jit(solution)/shard_map/project/pallas_call | solution.py:218
  2.9 0.0 copy-start
  2.9 0.0 copy-start.1
  3.0 0.0 copy-start.2
  3.0 0.0 copy-start.3
  3.0 0.0 copy-start.4
  3.0 0.0 copy-start.5
  3.0 0.0 copy-start.6
  3.0 48.4 %all_to_all.10 = bf16[128,9,4,128]{3,2,1,0:T(4,128)(2,1)S(1)} all-to-all(bf16[128,9,4,128]{3,2,1,0:T(4,128)(2,1)S(1)} %bitcast.14), channel_id=1, replica_groups=mesh['y'=4,'xl'=2,'z'=8,'xh'=2,'core'=2] {'y','xl','z','xh'}, dimensions={0} | all-to-all | bytes 2359296 | tf_op jit(solution)/shard_map/all_to_all | solution.py:242
  51.4 0.0 collective-permute-start
  51.4 0.0 copy-done
  51.4 0.0 copy-done.1
  51.4 0.0 copy-done.2
  51.4 0.0 copy-done.3
  51.4 0.0 copy-done.4
  51.4 0.0 copy-done.5
  51.4 0.0 copy-done.6
  51.4 1.9 %product_own.1 = (f32[512,1024]{1,0:T(8,128)S(1)}, f32[2304,128]{1,0:T(8,128)S(1)}, f32[128,128]{1,0:T(8,128)S(1)}, f32[128,128]{1,0:T(8,128)S(1)}, bf16[128,128]{1,0:T(8,128)(2,1)S(1)}) custom-call(s32[1]{0:T(128)} %bitcast.core, bf16[4608,128]{1,0:T(8,128)(2,1)S(1)} %bitcast.13, bf16[2304,128]{1,0:T(8,128)(2,1)S(1)} %bitcast.16, f32[1,128]{1,0:T(1,128)S(1)} %bitcast.21, ...), custom_call_target="tpu_custom_call" | custom-call | flops 400000000 | bytes 4000000 | tf_op jit(solution)/shard_map/product_own/pallas_call | solution.py:245
  53.4 0.8 collective-permute-done
  54.2 1.6 %product_other.1 = bf16[2304,128]{1,0:T(8,128)(2,1)S(1)} custom-call(s32[1]{0:T(128)} %bitcast.core, bf16[4608,128]{1,0:T(8,128)(2,1)S(1)} %bitcast.19, f32[512,1024]{1,0:T(8,128)S(1)} %get-tuple-element.10.total), custom_call_target="tpu_custom_call" | custom-call | tf_op jit(solution)/shard_map/product_other/pallas_call | solution.py:271
  55.9 26.4 %all_to_all.11 = bf16[128,9,2,128]{3,2,1,0:T(2,128)(2,1)S(1)} all-to-all(bf16[128,9,2,128]{3,2,1,0:T(2,128)(2,1)S(1)} %bitcast.18), channel_id=1, replica_groups=mesh['y'=4,'xl'=2,'z'=8,'xh'=2,'core'=2] {'xl','y','z','xh'}, dimensions={0} | all-to-all | bytes 1179648 | tf_op jit(solution)/shard_map/all_to_all | solution.py:283
  82.3 1.7 %finish.1 = bf16[2304,128]{1,0:T(8,128)(2,1)} custom-call(bf16[2304,128]{1,0:T(8,128)(2,1)S(1)} %bitcast.17, f32[2304,128]{1,0:T(8,128)S(1)} %get-tuple-element.11.gate, f32[128,128]{1,0:T(8,128)S(1)} %get-tuple-element.12.gain, f32[128,128]{1,0:T(8,128)S(1)} %get-tuple-element.13.bias, bf16[128,128]{1,0:T(8,128)(2,1)S(1)} %get-tuple-element.14.weight), custom_call_target="tpu_custom_call" | custom-call | tf_op jit(solution)/shard_map/finish/pallas_call | solution.py:284
Async XLA Ops:
  2.9 48.5 %copy-start = (bf16[96,24,128]{2,1,0:T(8,128)(2,1)S(1)}, bf16[96,24,128]{2,1,0:T(8,128)(2,1)}, u32[]{:S(2)}) copy-start(bf16[96,24,128]{2,1,0:T(8,128)(2,1)} %param.9) | copy-start | bytes 1769476
  2.9 48.5 %copy-start.1 = (bf16[128,128]{1,0:T(8,128)(2,1)S(1)}, bf16[128,128]{1,0:T(8,128)(2,1)}, u32[]{:S(2)}) copy-start(bf16[128,128]{1,0:T(8,128)(2,1)} %gate_weight.1) | copy-start | bytes 98308
  3.0 48.4 %copy-start.2 = (bf16[128,128]{1,0:T(8,128)(2,1)S(1)}, bf16[128,128]{1,0:T(8,128)(2,1)}, u32[]{:S(2)}) copy-start(bf16[128,128]{1,0:T(8,128)(2,1)} %weight.3) | copy-start | bytes 98308
  3.0 48.4 %copy-start.3 = (f32[128]{0:T(128)S(1)}, f32[128]{0:T(128)}, u32[]{:S(2)}) copy-start(f32[128]{0:T(128)} %param.11) | copy-start | bytes 1540
  3.0 48.4 %copy-start.4 = (f32[128]{0:T(128)S(1)}, f32[128]{0:T(128)}, u32[]{:S(2)}) copy-start(f32[128]{0:T(128)} %param.12) | copy-start | bytes 1540
  3.0 48.4 %copy-start.5 = (f32[128]{0:T(128)S(1)}, f32[128]{0:T(128)}, u32[]{:S(2)}) copy-start(f32[128]{0:T(128)} %param.15) | copy-start | bytes 1540
  3.0 48.4 %copy-start.6 = (f32[128]{0:T(128)S(1)}, f32[128]{0:T(128)}, u32[]{:S(2)}) copy-start(f32[128]{0:T(128)} %param.16) | copy-start | bytes 1540
  51.4 2.8 %collective-permute-start = (bf16[128,9,4,128]{3,2,1,0:T(4,128)(2,1)S(1)}, bf16[128,9,4,128]{3,2,1,0:T(4,128)(2,1)S(1)}, u32[]{:S(2)}, u32[]{:S(2)}) collective-permute-start(bf16[128,9,4,128]{3,2,1,0:T(4,128)(2,1)S(1)} %all_to_all.10), channel_id=1, source_target_pairs={{0,1},{1,0},{2,3},{3,2},{4,5},{5,4},{6,7},{7,6},{8,9},{9,8},{10,11... | collective-permute-start | bytes 3538952 | tf_op jit(solution)/shard_map/ppermute | solution.py:243

commit v10 on v7

--- a/solution.py
+++ b/solution.py
@@ -187,7 +187,7 @@
                 out[pl.ds((first + low - start) * COLS + BACK + row % 6, high - low, stride=COLS), :] = (
                     mixed[ROWS + low - 32 * group : ROWS + high - 32 * group]
                 )
-    parts = 4
+    parts = 2
     step = TOKENS // parts
     copies = []
     for part in range(parts):
@@ -288,7 +288,7 @@
             pltpu.VMEM((CH * BACK + BACK, CH), F32),
             pltpu.VMEM((TOKENS + COLS, CH), F32),
             pltpu.VMEM((TOKENS, CH), BF),
-            pltpu.SemaphoreType.DMA((4,)),
+            pltpu.SemaphoreType.DMA((2,)),
         ],
         compiler_params=PARAMS,
         name="finish",

time: 84.5 us -> 84.5 us (level)
  no operation moved by 1% of the time
where the time goes in v10:
time: 84.5 us; the launch traced here: 83.9 us
  blocking collectives  74.8 us (89%)
  Pallas kernels  7.75 us (9%)
  waiting for transfers between devices  1.27 us (2%)
    all_to_all x1, blocking collectives, body(): own = lax.all_to_all(sent.reshape(CH, 9, 4, CH), OUTWARD, 0, 0, tiled=True)  48.4 us
    all_to_all x1, blocking collectives, body(): tri = lax.all_to_all(tri.reshape(CH, 9, 2, CH), HOMEWARD, 0, 0, tiled=True)  26.5 us
    pallas_call x1, Pallas kernels, body(): pl.pallas_call(project_kernel, out_shape=(pltpu.VMEM((CH * SENT, CH), BF)...  2.93 us
  transfers between devices with their start and end apart: 1, of which 1 were waited for; matrix products, arithmetic and copies ran while one was open for 0% of the time, Pallas kernels for 2%

profile of v10, /device:TPU:32, one launch (start us, length us, event | category | flops | bytes accessed | tf_op | source)
XLA Modules:
  0.0 83.9 jit_solution(16281143741790595655)
XLA Ops:
  0.0 2.9 %project.1 = (bf16[4608,128]{1,0:T(8,128)(2,1)S(1)}, bf16[2304,128]{1,0:T(8,128)(2,1)S(1)}) custom-call(bf16[2304,128]{1,0:T(8,128)(2,1)} %bitcast.20, s32[24,96]{1,0:T(8,128)} %bitcast.21, f32[1,128]{1,0:T(1,128)} %bitcast.22, f32[1,128]{1,0:T(1,128)} %bitcast.23, bf16[128,512]{1,0:T(8,128)(2,1)} %weight.2), custom_call_target="tpu_custom_call" | custom-call | tf_op jit(solution)/shard_map/project/pallas_call | solution.py:215
  2.9 0.0 copy-start
  2.9 0.0 copy-start.1
  3.0 0.0 copy-start.2
  3.0 0.0 copy-start.3
  3.0 48.4 %all_to_all.10 = bf16[128,9,4,128]{3,2,1,0:T(4,128)(2,1)S(1)} all-to-all(bf16[128,9,4,128]{3,2,1,0:T(4,128)(2,1)S(1)} %bitcast.16), channel_id=1, replica_groups=mesh['y'=4,'xl'=2,'z'=8,'xh'=2,'core'=2] {'y','xl','z','xh'}, dimensions={0} | all-to-all | bytes 2359296 | tf_op jit(solution)/shard_map/all_to_all | solution.py:242
  51.4 0.0 collective-permute-start
  51.4 0.0 copy-done
  51.4 0.0 copy-done.1
  51.4 0.0 copy-done.2
  51.4 0.0 copy-done.3
  51.4 1.5 %product_own.1 = (f32[512,1024]{1,0:T(8,128)S(1)}, f32[2304,128]{1,0:T(8,128)S(1)}, f32[128,128]{1,0:T(8,128)S(1)}, f32[128,128]{1,0:T(8,128)S(1)}, bf16[128,128]{1,0:T(8,128)(2,1)S(1)}) custom-call(s32[1]{0:T(128)} %bitcast.core, bf16[4608,128]{1,0:T(8,128)(2,1)S(1)} %bitcast.13, bf16[2304,128]{1,0:T(8,128)(2,1)S(1)} %get-tuple-element.13.normed, ...), custom_call_target="tpu_custom_call" | custom-call | flops 400000000 | bytes 4000000 | tf_op jit(solution)/shard_map/product_own/pallas_call | solution.py:245
  52.9 1.3 %collective-permute-done = bf16[128,9,4,128]{3,2,1,0:T(4,128)(2,1)S(1)} collective-permute-done((bf16[128,9,4,128]{3,2,1,0:T(4,128)(2,1)S(1)}, bf16[128,9,4,128]{3,2,1,0:T(4,128)(2,1)S(1)}, u32[]{:S(2)}, u32[]{:S(2)}) %collective-permute-start) | collective-permute-done | bytes 1179680 | tf_op jit(solution)/shard_map/ppermute | solution.py:243
  54.2 1.6 %product_other.1 = bf16[2304,128]{1,0:T(8,128)(2,1)S(1)} custom-call(s32[1]{0:T(128)} %bitcast.core, bf16[4608,128]{1,0:T(8,128)(2,1)S(1)} %bitcast.17, f32[512,1024]{1,0:T(8,128)S(1)} %get-tuple-element.14.total), custom_call_target="tpu_custom_call" | custom-call | tf_op jit(solution)/shard_map/product_other/pallas_call | solution.py:269
  55.8 26.5 %all_to_all.11 = bf16[128,9,2,128]{3,2,1,0:T(2,128)(2,1)S(1)} all-to-all(bf16[128,9,2,128]{3,2,1,0:T(2,128)(2,1)S(1)} %bitcast.15), channel_id=1, replica_groups=mesh['y'=4,'xl'=2,'z'=8,'xh'=2,'core'=2] {'xl','y','z','xh'}, dimensions={0} | all-to-all | bytes 1179648 | tf_op jit(solution)/shard_map/all_to_all | solution.py:281
  82.3 1.7 %finish.1 = bf16[2304,128]{1,0:T(8,128)(2,1)} custom-call(bf16[2304,128]{1,0:T(8,128)(2,1)S(1)} %bitcast.14, f32[2304,128]{1,0:T(8,128)S(1)} %get-tuple-element.15.gate, f32[128,128]{1,0:T(8,128)S(1)} %get-tuple-element.16.gain, f32[128,128]{1,0:T(8,128)S(1)} %get-tuple-element.17.bias, bf16[128,128]{1,0:T(8,128)(2,1)S(1)} %get-tuple-element.18.weight), custom_call_target="tpu_custom_call" | custom-call | tf_op jit(solution)/shard_map/finish/pallas_call | solution.py:282
Async XLA Ops:
  2.9 48.4 %copy-start = (bf16[128,128]{1,0:T(8,128)(2,1)S(1)}, bf16[128,128]{1,0:T(8,128)(2,1)}, u32[]{:S(2)}) copy-start(bf16[128,128]{1,0:T(8,128)(2,1)} %gate_weight.1) | copy-start | bytes 98308
  2.9 48.4 %copy-start.1 = (bf16[128,128]{1,0:T(8,128)(2,1)S(1)}, bf16[128,128]{1,0:T(8,128)(2,1)}, u32[]{:S(2)}) copy-start(bf16[128,128]{1,0:T(8,128)(2,1)} %weight.3) | copy-start | bytes 98308
  3.0 48.4 %copy-start.2 = (f32[128]{0:T(128)S(1)}, f32[128]{0:T(128)}, u32[]{:S(2)}) copy-start(f32[128]{0:T(128)} %param.15) | copy-start | bytes 1540
  3.0 48.4 %copy-start.3 = (f32[128]{0:T(128)S(1)}, f32[128]{0:T(128)}, u32[]{:S(2)}) copy-start(f32[128]{0:T(128)} %param.16) | copy-start | bytes 1540
  51.4 2.8 %collective-permute-start = (bf16[128,9,4,128]{3,2,1,0:T(4,128)(2,1)S(1)}, bf16[128,9,4,128]{3,2,1,0:T(4,128)(2,1)S(1)}, u32[]{:S(2)}, u32[]{:S(2)}) collective-permute-start(bf16[128,9,4,128]{3,2,1,0:T(4,128)(2,1)S(1)} %all_to_all.10), channel_id=1, source_target_pairs={{0,1},{1,0},{2,3},{3,2},{4,5},{5,4},{6,7},{7,6},{8,9},{9,8},{10,11... | collective-permute-start | bytes 3538952 | tf_op jit(solution)/shard_map/ppermute | solution.py:243
